TPU v7x, 128 devices: a whole 4x4x4 slice. The times are simulated.
128 devices in a mesh: row: 8 (over y, core), col: 16 (over z, x).
Axes of the slice: x: 4, y: 4, z: 4, core: 2. Of those that a mesh axis runs over, the one named last changes fastest.
Arguments:
- waveforms: bfloat16 [128, 3, 160, 1024], P(('row', 'col')), may hold values from -600 to 600, as said below
- availability: int32 [128, 2], P(('row', 'col')), may hold values from 0 to 160, as said below
- pair_slot: int32 [128, 128], replicated, may hold values from 0 to 16383, as said below
- old_stack: float32 [16384, 3, 3, 512], P(('row', 'col')), may hold values from -1.8 to 1.8
Outputs:
- new_stack: float32 [16384, 3, 3, 512], P(('row', 'col'))
Inputs may be any that keep to these rules, and one draw needn't show every extreme that they name: waveforms[s, c, g, n] lies in the stated range. Station s has data in segments availability[s, 0] to availability[s, 1] - 1, with availability[s, 0] < 80 < availability[s, 1]. pair_slot holds every number of 0 .. 16383 once; its owner is pair_slot // 128. Pair a, b belongs to tile (a // 16) * 16 + b % 16. At most 2 pairs of one tile have one owner, and some tile and owner reach it; the number of pairs of tile d with owner o depends only on (o - d) modulo 128.
All inputs are finite; a program needn't handle non-finite values.
Results may differ from a plain program's by a relative error of at most 0.008.
Values may be sent and summed in bfloat16 or wider, within the bound.
No kernel may reach another device: no remote copies, remote signals or barrier semaphores. Data moves between devices by JAX's collectives and lax.ppermute only.
A program may use at most 256 MiB of HBM per device.

v0:
```python
import math

import jax
import jax.numpy as jnp
from jax import lax
from jax.sharding import PartitionSpec as P

ST_DEV = 1
SEGMENTS = 160
COMPONENTS = 3
SAMPLES = 1024
LAG_BINS = 512
BAND_HALF = 64
FREQ_BINS = 512
SEND_MOST = 2


EPSILON = 1e-06


def dft_table():
    sample_ids = jnp.arange(SAMPLES, dtype=jnp.int32)
    bin_ids = jnp.arange(FREQ_BINS, dtype=jnp.int32)
    turns = (sample_ids[:, None] * bin_ids[None, :] % SAMPLES).astype(jnp.float32) * (
        2.0 * math.pi / SAMPLES
    )
    return jnp.concatenate([jnp.cos(turns), -jnp.sin(turns)], axis=1).astype(jnp.bfloat16)


def band_table():
    bin_ids = jnp.arange(FREQ_BINS, dtype=jnp.int32)
    near_bins = (jnp.abs(bin_ids[:, None] - bin_ids[None, :]) <= BAND_HALF).astype(jnp.float32)
    return near_bins / jnp.sum(near_bins, axis=0, keepdims=True)


def lag_table():
    bin_ids = jnp.arange(FREQ_BINS, dtype=jnp.int32)
    lag_ids = jnp.arange(LAG_BINS, dtype=jnp.int32) - LAG_BINS // 2
    turns = (bin_ids[:, None] * lag_ids[None, :] % SAMPLES).astype(jnp.float32) * (
        2.0 * math.pi / SAMPLES
    )
    weight = jnp.where(bin_ids == 0, 1.0, 2.0).astype(jnp.float32) / math.sqrt(FREQ_BINS)
    return jnp.concatenate(
        [weight[:, None] * jnp.cos(turns), -weight[:, None] * jnp.sin(turns)], axis=0
    ).astype(jnp.bfloat16)


def segment_mask(availability):
    segment_ids = jnp.arange(SEGMENTS, dtype=jnp.int32)
    inside = (segment_ids[None, :] >= availability[:, 0:1]) & (
        segment_ids[None, :] < availability[:, 1:2]
    )
    return inside.astype(jnp.float32)


def whiten(waveforms, mask):
    station_count = waveforms.shape[0]
    flat_waves = waveforms.reshape(-1, SAMPLES)
    spectrum = jnp.dot(flat_waves, dft_table(), preferred_element_type=jnp.float32)
    real_part = spectrum[:, :FREQ_BINS]
    imag_part = spectrum[:, FREQ_BINS:]
    smooth = jnp.dot(
        real_part * real_part + imag_part * imag_part, band_table(), precision=lax.Precision.HIGHEST
    )
    factor = lax.rsqrt(smooth + EPSILON).reshape(station_count, COMPONENTS, SEGMENTS, 1, FREQ_BINS)
    factor = factor * mask[:, None, :, None, None]
    shaped = spectrum.reshape(station_count, COMPONENTS, SEGMENTS, 2, FREQ_BINS) * factor
    return jnp.transpose(shaped, (0, 1, 3, 2, 4)).astype(jnp.bfloat16)


def tile_partial(row_panel, row_mask, col_panel, col_mask, row_ids, col_ids):
    row_count = row_panel.shape[0]
    col_count = col_panel.shape[0]
    folded = row_panel.reshape(row_count, COMPONENTS, 2 * SEGMENTS, FREQ_BINS)
    turned = jnp.concatenate([row_panel[:, :, 1], -row_panel[:, :, 0]], axis=2)
    col_folded = col_panel.reshape(col_count, COMPONENTS, 2 * SEGMENTS, FREQ_BINS)
    real_cross = jnp.einsum(
        "ackf,bdkf->bacdf", folded, col_folded, preferred_element_type=jnp.float32
    )
    imag_cross = jnp.einsum(
        "ackf,bdkf->bacdf", turned, col_folded, preferred_element_type=jnp.float32
    )
    cross_spec = jnp.concatenate([real_cross, imag_cross], axis=4).astype(jnp.bfloat16)
    lagged = jnp.dot(
        cross_spec.reshape(-1, 2 * FREQ_BINS), lag_table(), preferred_element_type=jnp.float32
    )
    lagged = lagged.reshape(col_count, row_count, COMPONENTS * COMPONENTS * LAG_BINS)
    counts = jnp.dot(col_mask, row_mask.T, precision=lax.Precision.HIGHEST)
    keep_pair = (col_ids[:, None] != row_ids[None, :]).astype(jnp.float32)
    return lagged * (keep_pair / counts)[:, :, None]


def local(waveforms, availability, pair_slot, old_stack):
    row_index = lax.axis_index("row")
    col_index = lax.axis_index("col")
    row_tiles = lax.axis_size("row")
    col_tiles = lax.axis_size("col")
    row_block = ST_DEV * col_tiles
    col_block = ST_DEV * row_tiles
    row_width = COMPONENTS * COMPONENTS * LAG_BINS
    own_mask = segment_mask(availability)
    own_mask_half = own_mask.astype(jnp.bfloat16)
    row_ids = row_index * row_block + jnp.arange(row_block, dtype=jnp.int32)
    panels = {}
    own_panel = whiten(waveforms, own_mask)
    row_panel, row_mask = (
        lax.all_gather(own_panel, "col", axis=0, tiled=True),
        lax.all_gather(own_mask_half, "col", axis=0, tiled=True),
    )
    panels["row_panel"] = row_panel
    panels["row_mask"] = row_mask.astype(jnp.float32)
    col_panel = lax.all_gather(own_panel, "row", axis=0, tiled=True)
    col_local = jnp.arange(col_panel.shape[0], dtype=jnp.int32)
    col_ids = col_local // ST_DEV * row_block + col_index * ST_DEV + col_local % ST_DEV
    tile_rows = tile_partial(
        panels["row_panel"],
        panels["row_mask"],
        col_panel,
        lax.all_gather(own_mask_half, "row", axis=0, tiled=True).astype(jnp.float32),
        row_ids,
        col_ids,
    )
    tile_slots = lax.dynamic_slice_in_dim(pair_slot, row_index * row_block, row_block, 0)
    tile_slots = tile_slots.reshape(row_block, row_tiles, col_tiles, ST_DEV)
    tile_slots = lax.dynamic_index_in_dim(tile_slots, col_index, 2, keepdims=False)
    tile_slots = tile_slots.reshape(row_block, col_block).T.reshape(-1)
    per_owner = old_stack.shape[0]
    owners_total = row_tiles * col_tiles
    owner_ids = tile_slots // per_owner
    slot_within = tile_slots % per_owner
    hit_table = (owner_ids[:, None] == jnp.arange(owners_total, dtype=jnp.int32)[None, :]).astype(
        jnp.int32
    )
    send_rank = jnp.sum(jnp.cumsum(hit_table, axis=0) * hit_table, axis=1) - 1
    target_rows = owner_ids * SEND_MOST + send_rank
    outgoing = (
        jnp.zeros((owners_total * SEND_MOST, row_width), jnp.float32)
        .at[target_rows]
        .set(tile_rows.reshape(-1, row_width))
    )
    labels = (
        jnp.full((owners_total * SEND_MOST,), per_owner, jnp.float32)
        .at[target_rows]
        .set(slot_within.astype(jnp.float32))
    )
    incoming, arrived = (
        lax.all_to_all(outgoing, ("row", "col"), split_axis=0, concat_axis=0, tiled=True),
        lax.all_to_all(labels, ("row", "col"), split_axis=0, concat_axis=0, tiled=True),
    )
    arrived = arrived.astype(jnp.int32)
    new_stack = old_stack.reshape(per_owner, row_width).at[arrived].add(incoming, mode="drop")
    return new_stack.reshape(old_stack.shape)


def solution(mesh):
    return jax.shard_map(
        local,
        mesh=mesh,
        in_specs=(
            P(("row", "col"), None, None, None),
            P(("row", "col"), None),
            P(),
            P(("row", "col"), None, None, None),
        ),
        out_specs=P(("row", "col"), None, None, None),
        check_vma=False,
    )
```

profile of v0, /device:TPU:1, one launch (start us, length us, event | category | flops | bytes accessed | tf_op | source)
XLA Modules:
  0.0 468.8 jit_solution(14449937608757424086)
XLA Ops:
  6.5 8.5 %negate_convert_fusion = (bf16[1024,512]{1,0:T(8,128)(2,1)S(1)}, bf16[1024,512]{1,0:T(8,128)(2,1)S(1)}) fusion(), kind=kLoop, calls=%fused_computation.27 | loop fusion | flops 8912896 | bytes 2097152 | tf_op jit(solution)/shard_map/convert.9
  16.6 2.5 fusion.21
  19.0 3.0 reshape.267
  22.0 3.3 fusion.24
  32.2 11.5 %all-to-all-start = ((f32[128,2,1]{1,2,0:T(1,128)}), f32[128,2,1]{1,2,0:T(1,128)S(1)}, u32[]{:S(2)}, u32[]{:S(2)}) async-start(f32[128,2,1]{1,2,0:T(1,128)} %bitcast.6), calls=%async_computation | async-start | bytes 131072 | tf_op jit(solution)/shard_map/all_to_all | solution.py:148
  44.9 10.9 %all-gather = bf16[8,1,160]{2,1,0:T(2,128)(2,1)S(1)} all-gather(bf16[1,1,160]{2,1,0:T(2,128)(2,1)S(1)} %convert_bitcast_fusion.2), channel_id=1, replica_groups=mesh['row'=8,'col'=16] {'row'}, dimensions={0}, use_global_device_ids=true | all-gather | bytes 2880 | tf_op jit(solution)/shard_map/all_gather | solution.py:119
  55.8 21.4 %all-gather.1 = bf16[16,1,160]{2,1,0:T(2,128)(2,1)S(1)} all-gather(bf16[1,1,160]{2,1,0:T(2,128)(2,1)S(1)} %convert_bitcast_fusion.2), channel_id=1, replica_groups=mesh['row'=8,'col'=16] {'col'}, dimensions={0}, use_global_device_ids=true | all-gather | bytes 5440 | tf_op jit(solution)/shard_map/all_gather | solution.py:108
  77.4 4.4 multiply_convert_fusion.1
  81.8 12.9 %copy.63 = bf16[8,3,320,512,1]{2,0,4,1,3:T(8,128)(2,1)} copy(bf16[8,3,320,512,1]{3,2,1,0,4:T(8,128)(2,1)} %bitcast.59) | data formatting | bytes 15728640 | tf_op jit(solution)/shard_map/reshape | solution.py:76
  94.8 93.2 %all-gather.7.cloned.1.call-done = bf16[16,3,2,160,512]{4,3,2,1,0:T(8,128)(2,1)} async-done(((bf16[1,3,2,160,512]{4,3,2,1,0:T(8,128)(2,1)}), bf16[16,3,2,160,512]{4,3,2,1,0:T(8,128)(2,1)}) %all-gather.7.cloned.1.call-update) | async-done | bytes 15728656 | tf_op jit(solution)/shard_map/all_gather | solution.py:107
  188.0 11.2 %fusion.54 = (bf16[16,3,1,160,512]{4,3,2,1,0:T(8,128)(2,1)}, bf16[16,3,1,160,512]{4,3,2,1,0:T(8,128)(2,1)}) fusion(bf16[16,3,2,160,512]{4,3,2,1,0:T(8,128)(2,1)} %all-gather.7.cloned.1.call-done), kind=kLoop, calls=%fused_computation.102 | loop fusion | bytes 31457280 | tf_op jit(solution)/shard_map/slice | solution.py:75
  199.2 17.6 %copy.76 = bf16[16,3,1,160,512]{3,0,1,4,2:T(8,128)(2,1)} copy(bf16[16,3,1,160,512]{4,3,2,1,0:T(8,128)(2,1)} %get-tuple-element.6) | data formatting | bytes 15728640
  216.8 10.6 %negate_bitcast_fusion = bf16[16,3,160,512]{2,0,1,3:T(8,128)(2,1)} fusion(bf16[16,3,1,160,512]{3,0,1,4,2:T(8,128)(2,1)} %copy.76), kind=kLoop, calls=%fused_computation.7 | loop fusion | flops 3932160 | bytes 15728640 | tf_op jit(solution)/shard_map/neg | solution.py:75
  227.4 17.6 %copy.75 = bf16[16,3,1,160,512]{3,0,1,4,2:T(8,128)(2,1)} copy(bf16[16,3,1,160,512]{4,3,2,1,0:T(8,128)(2,1)} %get-tuple-element.5) | data formatting | bytes 15728640
  245.1 29.5 %convert_bitcast_fusion = bf16[8,16,3,3,512]{1,0,2,3,4:T(8,128)(2,1)} fusion(bf16[8,3,320,512,1]{2,0,4,1,3:T(8,128)(2,1)} %copy.63, bf16[16,3,160,512]{2,0,1,3:T(8,128)(2,1)} %negate_bitcast_fusion, bf16[16,3,160,512]{2,0,1,3:T(8,128)(2,1)} %bitcast.56), kind=kOutput, calls=%fused_computation.8 | convolution fusion | flops 409534464 | bytes 24772608 | tf_op jit(solution)/shard_map/ackf,bdkf->bacdf/dot_general | solution.py:80
  274.6 11.9 %copy.59 = bf16[8,16,3,3,512]{4,3,2,1,0:T(4,128)(2,1)S(1)} copy(bf16[8,16,3,3,512]{1,0,2,3,4:T(8,128)(2,1)} %convert_bitcast_fusion) | data formatting | bytes 2359296 | tf_op jit(solution)/shard_map/ackf,bdkf->bacdf/transpose | solution.py:80
  286.6 2.2 concatenate.23
  288.8 24.2 %copy.64 = bf16[16,3,320,512,1]{2,0,1,4,3:T(8,128)(2,1)} copy(bf16[16,3,320,512,1]{3,2,1,0,4:T(8,128)(2,1)} %bitcast.55) | data formatting | bytes 31457280 | tf_op jit(solution)/shard_map/reshape | solution.py:74
  313.0 31.0 %convert_bitcast_fusion.1 = bf16[8,16,3,3,512]{1,0,2,3,4:T(8,128)(2,1)} fusion(bf16[8,3,320,512,1]{2,0,4,1,3:T(8,128)(2,1)} %copy.63, bf16[16,3,320,512,1]{2,0,1,4,3:T(8,128)(2,1)} %copy.64), kind=kOutput, calls=%fused_computation.9 | convolution fusion | flops 378077184 | bytes 24772608 | tf_op jit(solution)/shard_map/ackf,bdkf->bacdf/dot_general | solution.py:77
  344.0 11.9 %copy.55 = bf16[8,16,3,3,512]{4,3,2,1,0:T(4,128)(2,1)S(1)} copy(bf16[8,16,3,3,512]{1,0,2,3,4:T(8,128)(2,1)} %convert_bitcast_fusion.1) | data formatting | bytes 2359296 | tf_op jit(solution)/shard_map/ackf,bdkf->bacdf/transpose | solution.py:77
  355.9 2.2 concatenate.21
  358.1 4.4 fusion.3
  362.6 2.4 reshape.271
  365.0 4.5 scatter_custom_fusion.1
  369.5 6.3 %all_to_all.16 = f32[128,2,4608]{2,1,0:T(2,128)} reshape(f32[256,4608]{1,0:T(8,128)} %scatter_custom_fusion.1) | data formatting | bytes 9437184 | tf_op jit(solution)/shard_map/all_to_all | solution.py:147
  375.8 8.7 %all-to-all-start.1 = ((f32[128,2,4608]{2,1,0:T(2,128)}), f32[128,2,4608]{2,1,0:T(2,128)}, u32[]{:S(2)}, u32[]{:S(2)}) async-start(f32[128,2,4608]{2,1,0:T(2,128)} %all_to_all.16), calls=%async_computation.1 | async-start | bytes 9437184 | tf_op jit(solution)/shard_map/all_to_all | solution.py:147
  386.4 2.0 copy.60
  388.8 52.3 %all-to-all-done.1 = f32[128,2,4608]{2,1,0:T(2,128)} async-done(((f32[128,2,4608]{2,1,0:T(2,128)}), f32[128,2,4608]{2,1,0:T(2,128)}, u32[]{:S(2)}, u32[]{:S(2)}) %all-to-all-start.1) | async-done | bytes 4718624 | tf_op jit(solution)/shard_map/all_to_all | solution.py:147
  441.1 6.5 %reshape.293 = f32[256,4608]{1,0:T(8,128)} reshape(f32[128,2,4608]{2,1,0:T(2,128)} %all-to-all-done.1) | data formatting | bytes 9437184 | tf_op jit(solution)/shard_map/all_to_all | solution.py:147
  447.7 8.9 %scatter_fusion = f32[128,4608]{1,0:T(8,128)S(1)} fusion(f32[128,4608]{1,0:T(8,128)S(1)} %copy.60, s32[256]{0:T(256)S(1)} %bitcast.63, f32[256,4608]{1,0:T(8,128)} %reshape.293), kind=kCustom, calls=%fused_computation.2 | custom fusion | flops 1179648 | bytes 14156800 | tf_op jit(solution)/shard_map/scatter-add | solution.py:151
  456.6 2.0 copy.61
  458.6 3.1 copy.62
  (41 shorter events, 11.9 us)
Async XLA Ops:
  6.5 10.0 %copy-start = (bf16[1,3,160,1024]{3,2,1,0:T(8,128)(2,1)S(1)}, bf16[1,3,160,1024]{3,2,1,0:T(8,128)(2,1)}, u32[]{:S(2)}) copy-start(bf16[1,3,160,1024]{3,2,1,0:T(8,128)(2,1)} %param.4) | copy-start | bytes 2949124
  6.5 75.3 %all-gather.5.cloned.1.call-start = ((), (), s32[]{:S(2)}) async-start(), calls=%async_computation.2 | async-start | bytes 8847360 | tf_op jit(solution)/shard_map/all_gather | solution.py:112
  28.0 160.0 %all-gather.7.cloned.1.call-start = ((), (), s32[]{:S(2)}) async-start(), calls=%async_computation.3 | async-start | bytes 16711680 | tf_op jit(solution)/shard_map/all_gather | solution.py:107
  32.2 343.6 %all-to-all-start = ((f32[128,2,1]{1,2,0:T(1,128)}), f32[128,2,1]{1,2,0:T(1,128)S(1)}, u32[]{:S(2)}, u32[]{:S(2)}) async-start(f32[128,2,1]{1,2,0:T(1,128)} %bitcast.6), calls=%async_computation | async-start | bytes 131072 | tf_op jit(solution)/shard_map/all_to_all | solution.py:148
  375.7 8.7 %copy-start.2 = (f32[128,3,3,512]{3,0,2,1:T(8,128)S(1)}, f32[128,3,3,512]{3,0,2,1:T(8,128)}, u32[]{:S(2)}) copy-start(f32[128,3,3,512]{3,0,2,1:T(8,128)} %param.7) | copy-start | bytes 7077892
  375.8 65.4 %all-to-all-start.1 = ((f32[128,2,4608]{2,1,0:T(2,128)}), f32[128,2,4608]{2,1,0:T(2,128)}, u32[]{:S(2)}, u32[]{:S(2)}) async-start(f32[128,2,4608]{2,1,0:T(2,128)} %all_to_all.16), calls=%async_computation.1 | async-start | bytes 9437184 | tf_op jit(solution)/shard_map/all_to_all | solution.py:147
  458.6 3.1 copy-start.1
Sparse Core Ops, SparseCore 0:
  28.1 51.9 all-gather.4
  82.2 105.7 all-gather.6
where the time goes:
time: 477 us; the launch traced here: 469 us
  waiting for transfers between devices  146 us (31%)
  local copies, waits for them, and re-layouts  144 us (30%)
  matrix products  70.9 us (15%)
  other arithmetic  41.6 us (9%)
  blocking collectives  32.3 us (7%)
  starting transfers between devices  20.2 us (4%)
  between operations  13.8 us (3%)
    all_gather x1, waiting for transfers between devices, local(): lax.all_gather(own_panel, 'col', axis=0, tiled=True)  93.2 us
    all_to_all x1, waiting for transfers between devices, local(): lax.all_to_all(outgoing, ('row', 'col'), split_axis=0, concat_axis=0, til...  52.3 us
    unnamed x9, local copies, waits for them, and re-layouts  37.2 us
    dot_general x1, matrix products, tile_partial(): jnp.einsum('ackf,bdkf->bacdf', folded, col_folded, preferred_element_type...  31 us
    dot_general x1, matrix products, tile_partial(): jnp.einsum('ackf,bdkf->bacdf', turned, col_folded, preferred_element_type...  29.5 us
    reshape x1, local copies, waits for them, and re-layouts, tile_partial(): folded = row_panel.reshape(row_count, COMPONENTS, 2 * SEGMENTS, FREQ_BINS)  24.2 us
    all_gather x1, blocking collectives, local(): lax.all_gather(own_mask_half, 'col', axis=0, tiled=True)  21.4 us
    another operation x2, other arithmetic  13 us
  transfers between devices with their start and end apart: 4, of which 2 were waited for; matrix products, arithmetic and copies ran while one was open for 44% of the time, Pallas kernels for 0%

commit v1 on v0

v1 whole, which is shorter than its diff:
```python
import functools
import math

import jax
import jax.numpy as jnp
import ml_dtypes
import numpy as np
from jax import lax
from jax.experimental import pallas as pl
from jax.experimental.pallas import tpu as pltpu
from jax.sharding import PartitionSpec as P

SEGMENTS = 160
COMPONENTS = 3
SAMPLES = 1024
LAG_BINS = 512
BAND_HALF = 64
FREQ_BINS = 512
DEVICES = 128
STATIONS = 128
PER_OWNER = 128
BINS = FREQ_BINS // DEVICES
PARTS = 2 * BINS
LANES = COMPONENTS * SEGMENTS
LANES_FULL = 512
PRODUCTS = COMPONENTS * COMPONENTS
VALUES = PRODUCTS * PARTS

EPSILON = 1e-06
VMEM_LIMIT = 56 * 1024 * 1024
NT = (((1,), (1,)), ((), ()))
TN = (((0,), (0,)), ((), ()))


def dft_table():
    turns = np.arange(FREQ_BINS)[:, None] * np.arange(SAMPLES)[None, :] % SAMPLES
    turns = turns.astype(np.float32) * np.float32(2.0 * math.pi / SAMPLES)
    table = np.concatenate([np.cos(turns), -np.sin(turns)], axis=0)
    return table.astype(ml_dtypes.bfloat16)


def band_tables():
    bin_ids = np.arange(FREQ_BINS)
    near = np.abs(bin_ids[:, None] - bin_ids[None, :]) <= BAND_HALF
    return near.astype(ml_dtypes.bfloat16), (1.0 / near.sum(axis=1, keepdims=True)).astype(np.float32)


def lag_table():
    bin_ids = np.arange(FREQ_BINS)
    lag_ids = np.arange(LAG_BINS) - LAG_BINS // 2
    turns = bin_ids[:, None] * lag_ids[None, :] % SAMPLES
    turns = turns.astype(np.float32) * np.float32(2.0 * math.pi / SAMPLES)
    weight = np.where(bin_ids == 0, 1.0, 2.0).astype(np.float32)[:, None] / np.float32(math.sqrt(FREQ_BINS))
    both = np.stack([weight * np.cos(turns), -weight * np.sin(turns)])
    both = both.reshape(2, DEVICES, BINS, LAG_BINS).transpose(1, 0, 2, 3)
    return both.reshape(2 * FREQ_BINS, LAG_BINS).astype(ml_dtypes.bfloat16)


def whiten_kernel(avail_ref, wave_ref, dft_ref, band_ref, share_ref, out_ref, wave_full):
    wave_full[:LANES] = wave_ref[...]
    wave_full[LANES:] = jnp.zeros((LANES_FULL - LANES, SAMPLES), jnp.bfloat16)
    waves = wave_full[...]
    real = lax.dot_general(dft_ref[:FREQ_BINS], waves, NT, preferred_element_type=jnp.float32)
    imag = lax.dot_general(dft_ref[FREQ_BINS:], waves, NT, preferred_element_type=jnp.float32)
    power = real * real + imag * imag
    high = power.astype(jnp.bfloat16)
    low = (power - high.astype(jnp.float32)).astype(jnp.bfloat16)
    band = band_ref[...]
    smooth = jnp.dot(band, high, preferred_element_type=jnp.float32) + jnp.dot(
        band, low, preferred_element_type=jnp.float32
    )
    lane = lax.broadcasted_iota(jnp.int32, (1, LANES_FULL), 1)
    segment = lane % SEGMENTS
    first, last = avail_ref[0, 0], avail_ref[0, 1]
    mask = ((segment >= first) & (segment < last) & (lane < LANES)).astype(jnp.float32)
    factor = lax.rsqrt(smooth * share_ref[...] + EPSILON) * mask
    spare = jnp.where(lane == LANES, first, jnp.where(lane == LANES + 1, last, 0)).astype(jnp.float32)
    real = (real * factor + spare).reshape(FREQ_BINS // 8, 8, LANES_FULL)
    imag = (imag * factor + spare).reshape(FREQ_BINS // 8, 8, LANES_FULL)
    lower = lax.broadcasted_iota(jnp.int32, (1, 8, 1), 1) < BINS
    out_ref[:, 0] = jnp.where(lower, real, pltpu.roll(imag, BINS, 1)).astype(jnp.bfloat16)
    out_ref[:, 1] = jnp.where(lower, pltpu.roll(real, BINS, 1), imag).astype(jnp.bfloat16)


def whiten(waves, availability):
    near, share = band_tables()
    out = pl.pallas_call(
        whiten_kernel,
        out_shape=jax.ShapeDtypeStruct((FREQ_BINS // 8, 2, PARTS, LANES_FULL), jnp.bfloat16),
        in_specs=[pl.BlockSpec(memory_space=pltpu.SMEM)] + [pl.BlockSpec(memory_space=pltpu.VMEM)] * 4,
        out_specs=pl.BlockSpec(memory_space=pltpu.VMEM),
        scratch_shapes=[pltpu.VMEM((LANES_FULL, SAMPLES), jnp.bfloat16)],
        compiler_params=pltpu.CompilerParams(vmem_limit_bytes=VMEM_LIMIT),
    )(availability, waves, jnp.asarray(dft_table()), jnp.asarray(near), jnp.asarray(share))
    return out.reshape(DEVICES, PARTS, LANES_FULL)


def cross_kernel(slot_ref, spec_ref, out_ref, spec_full, planes, turned, placed):
    wide = spec_ref[...].astype(jnp.float32).reshape(STATIONS * PARTS, LANES_FULL)
    tiles = LANES_FULL // 128
    for t in range(tiles):
        spec_full[t] = wide[:, t * 128 : (t + 1) * 128]

    def part(row):
        return jnp.concatenate(
            [spec_full[t, pl.ds(row, STATIONS, stride=PARTS), :] for t in range(tiles)], axis=1
        )

    head = part(0)
    first = jnp.broadcast_to(head[:, LANES : LANES + 1], (STATIONS, STATIONS))
    last = jnp.broadcast_to(head[:, LANES + 1 : LANES + 2], (STATIONS, STATIONS))
    counts = jnp.minimum(last, last.T) - jnp.maximum(first, first.T)
    one = lax.broadcasted_iota(jnp.int32, (STATIONS, STATIONS), 0)
    two = lax.broadcasted_iota(jnp.int32, (STATIONS, STATIONS), 1)
    scale = jnp.where(one == two, 0.0, 1.0 / counts)

    def fold(values):
        return jnp.concatenate(
            [values[:, c * SEGMENTS : (c + 1) * SEGMENTS] for c in range(COMPONENTS)], axis=0
        ).astype(jnp.bfloat16)

    def product(x, y):
        return lax.dot_general(x, y, NT, preferred_element_type=jnp.float32)

    for f in range(BINS):
        real, imag = fold(part(f)), fold(part(BINS + f))
        both = (product(real, real) + product(imag, imag), product(imag, real) - product(real, imag))
        for p in range(2):
            for c in range(COMPONENTS):
                for d in range(COMPONENTS):
                    plane = both[p][c * STATIONS : (c + 1) * STATIONS, d * STATIONS : (d + 1) * STATIONS]
                    row = (c * COMPONENTS + d) * PARTS + p * BINS + f
                    planes[pl.ds(row, STATIONS, stride=VALUES), :] = plane * scale

    def place(a, carry):
        turned[:, :VALUES] = planes[pl.ds(a * VALUES, VALUES), :].T
        for b in range(STATIONS):
            placed[pl.ds(slot_ref[a * STATIONS + b], 1), :] = turned[b : b + 1, :]
        return carry

    lax.fori_loop(0, STATIONS, place, 0)

    def finish(owner, carry):
        out_ref[owner] = placed[pl.ds(owner * PER_OWNER, PER_OWNER), :].T[:VALUES].astype(jnp.bfloat16)
        return carry

    lax.fori_loop(0, DEVICES, finish, 0)


def cross(slots, spectra):
    return pl.pallas_call(
        cross_kernel,
        out_shape=jax.ShapeDtypeStruct((DEVICES, VALUES, PER_OWNER), jnp.bfloat16),
        in_specs=[pl.BlockSpec(memory_space=pltpu.SMEM), pl.BlockSpec(memory_space=pltpu.VMEM)],
        out_specs=pl.BlockSpec(memory_space=pltpu.VMEM),
        scratch_shapes=[
            pltpu.VMEM((LANES_FULL // 128, STATIONS * PARTS, 128), jnp.float32),
            pltpu.VMEM((STATIONS * VALUES, STATIONS), jnp.float32),
            pltpu.VMEM((STATIONS, 128), jnp.float32),
            pltpu.VMEM((DEVICES * PER_OWNER, 128), jnp.float32),
        ],
        compiler_params=pltpu.CompilerParams(vmem_limit_bytes=VMEM_LIMIT),
    )(slots, spectra)


def lag_kernel(cross_ref, table_ref, old_ref, out_ref):
    row = pl.multiple_of(pl.program_id(0) * PARTS, PARTS)
    spectra = cross_ref[:, pl.ds(row, PARTS), :].reshape(2 * FREQ_BINS, PER_OWNER)
    lagged = lax.dot_general(spectra, table_ref[...], TN, preferred_element_type=jnp.float32)
    out_ref[0] = old_ref[0] + lagged


def lag(arrived, old_rows):
    return pl.pallas_call(
        lag_kernel,
        grid=(PRODUCTS,),
        out_shape=jax.ShapeDtypeStruct((PRODUCTS, PER_OWNER, LAG_BINS), jnp.float32),
        in_specs=[
            pl.BlockSpec((DEVICES, VALUES, PER_OWNER), lambda i: (0, 0, 0)),
            pl.BlockSpec((2 * FREQ_BINS, LAG_BINS), lambda i: (0, 0)),
            pl.BlockSpec((1, PER_OWNER, LAG_BINS), lambda i: (i, 0, 0)),
        ],
        out_specs=pl.BlockSpec((1, PER_OWNER, LAG_BINS), lambda i: (i, 0, 0)),
        compiler_params=pltpu.CompilerParams(vmem_limit_bytes=VMEM_LIMIT),
    )(arrived, jnp.asarray(lag_table()), old_rows)


def local(waveforms, availability, pair_slot, old_stack):
    axes = ("row", "col")
    spectra = whiten(waveforms.reshape(LANES, SAMPLES), availability)
    spectra = lax.all_to_all(spectra, axes, split_axis=0, concat_axis=0, tiled=True)
    crossed = cross(pair_slot.reshape(-1), spectra)
    arrived = lax.all_to_all(crossed, axes, split_axis=0, concat_axis=0, tiled=True)
    old_rows = jnp.transpose(old_stack, (1, 2, 0, 3)).reshape(PRODUCTS, PER_OWNER, LAG_BINS)
    new_rows = lag(arrived, old_rows).reshape(COMPONENTS, COMPONENTS, PER_OWNER, LAG_BINS)
    return jnp.transpose(new_rows, (2, 0, 1, 3))


def solution(mesh):
    return jax.shard_map(
        local,
        mesh=mesh,
        in_specs=(
            P(("row", "col"), None, None, None),
            P(("row", "col"), None),
            P(),
            P(("row", "col"), None, None, None),
        ),
        out_specs=P(("row", "col"), None, None, None),
        check_vma=False,
    )
```

time: 477 us -> 121 us (0.25); the launches traced: 469 us -> 121 us
  waiting for transfers between devices: 146 us -> 0 us
  local copies, waits for them, and re-layouts: 144 us -> 0 us
  matrix products: 70.9 us -> 0 us
  Pallas kernels: 0 us -> 52.4 us
  other arithmetic: 41.6 us -> 0 us
  blocking collectives: 32.3 us -> 68.5 us
  starting transfers between devices: 20.2 us -> 0 us
  between operations: 13.8 us -> 0.01 us
    all_gather x2 -> x0, waiting for transfers between devices: 93.3 us -> none  [the longest x1 93.2 us: local(): lax.all_gather(own_panel, 'col', axis=0, tiled=True)]
    dot_general x6 -> x0, matrix products: 70.9 us -> none  [the longest x1 31 us: tile_partial(): jnp.einsum('ackf,bdkf->bacdf', folded, col_folded, preferred_element_type...]
    all_to_all x0 -> x2, blocking collectives: none -> 68.5 us  [the longest x1 37.6 us: local(): lax.all_to_all(crossed, axes, split_axis=0, concat_axis=0, tiled=True)]
    pallas_call x0 -> x3, Pallas kernels: none -> 52.4 us  [the longest x1 38.4 us: cross(): pl.pallas_call(cross_kernel, out_shape=jax.ShapeDtypeStruct((DEVICES, VAL...]
    all_to_all x2 -> x0, waiting for transfers between devices: 52.3 us -> none  [the longest x1 52.3 us: local(): lax.all_to_all(outgoing, ('row', 'col'), split_axis=0, concat_axis=0, til...]
    reshape x9 -> x0, local copies, waits for them, and re-layouts: 47.9 us -> none  [the longest x1 24.2 us: tile_partial(): folded = row_panel.reshape(row_count, COMPONENTS, 2 * SEGMENTS, FREQ_BINS)]
    unnamed x9 -> x0, local copies, waits for them, and re-layouts: 37.2 us -> none
    all_gather x2 -> x0, blocking collectives: 32.3 us -> none  [the longest x1 21.4 us: local(): lax.all_gather(own_mask_half, 'col', axis=0, tiled=True)]
  transfers between devices with their start and end apart: 4 -> 0, of which waited for: 2 -> 0; matrix products, arithmetic and copies ran while one was open for 44% -> 0% of each run, Pallas kernels for 0% -> 0%
where the time goes in v1:
time: 121 us
  blocking collectives  68.5 us (57%)
  Pallas kernels  52.4 us (43%)
    pallas_call x1, Pallas kernels, cross(): pl.pallas_call(cross_kernel, out_shape=jax.ShapeDtypeStruct((DEVICES, VAL...  38.4 us
    all_to_all x1, blocking collectives, local(): lax.all_to_all(crossed, axes, split_axis=0, concat_axis=0, tiled=True)  37.6 us
    all_to_all x1, blocking collectives, local(): lax.all_to_all(spectra, axes, split_axis=0, concat_axis=0, tiled=True)  30.9 us
    pallas_call x1, Pallas kernels, lag(): pl.pallas_call(lag_kernel, grid=(PRODUCTS,), out_shape=jax.ShapeDtypeStru...  8.72 us
    pallas_call x1, Pallas kernels, whiten(): pl.pallas_call(whiten_kernel, out_shape=jax.ShapeDtypeStruct((FREQ_BINS /...  5.24 us

profile of v1, /device:TPU:1, one launch (start us, length us, event | category | flops | bytes accessed | tf_op | source)
XLA Modules:
  0.0 120.9 jit_solution(9017264068757943738)
XLA Ops:
  0.0 5.2 %shard_map.82 = bf16[64,2,8,512]{3,2,1,0:T(8,128)(2,1)} custom-call(s32[1,2]{1,0:T(1,128)} %avail_ref.1, bf16[480,1024]{1,0:T(8,128)(2,1)} %bitcast.11, bf16[1024,1024]{1,0:T(8,128)(2,1)} %constant.8.clone.dft_ref, bf16[512,512]{1,0:T(8,128)(2,1)} %constant.9.clone.band_ref, f32[512,1]{1,0:T(8,128)} %constant.10.clone.share_ref), custom_call_target="tpu_custom_call" | custom-call | tf_op jit(solution)/shard_map/pallas_call | solution.py:87
  5.2 30.9 %all_to_all.10.spec_ref = bf16[128,8,512]{2,1,0:T(8,128)(2,1)} all-to-all(bf16[128,8,512]{2,1,0:T(8,128)(2,1)} %bitcast.9), channel_id=1, replica_groups=mesh['row'=8,'col'=16] {'row','col'}, dimensions={0} | all-to-all | bytes 2097152 | tf_op jit(solution)/shard_map/all_to_all | solution.py:191
  36.1 38.4 %shard_map.83 = bf16[128,72,128]{2,1,0:T(8,128)(2,1)} custom-call(s32[16384]{0:T(1024)} %bitcast.12, bf16[128,8,512]{2,1,0:T(8,128)(2,1)} %all_to_all.10.spec_ref), custom_call_target="tpu_custom_call" | custom-call | tf_op jit(solution)/shard_map/pallas_call | solution.py:151
  74.6 37.6 %all_to_all.11.cross_ref = bf16[128,72,128]{2,1,0:T(8,128)(2,1)} all-to-all(bf16[128,72,128]{2,1,0:T(8,128)(2,1)} %shard_map.83), channel_id=1, replica_groups=mesh['row'=8,'col'=16] {'row','col'}, dimensions={0} | all-to-all | bytes 4718592 | tf_op jit(solution)/shard_map/all_to_all | solution.py:193
  112.1 8.7 %shard_map.84 = f32[9,128,512]{2,1,0:T(8,128)} custom-call(bf16[128,72,128]{2,1,0:T(8,128)(2,1)} %all_to_all.11.cross_ref, bf16[1024,512]{1,0:T(8,128)(2,1)} %constant.11.clone.table_ref, f32[9,128,512]{2,1,0:T(8,128)} %bitcast.10), custom_call_target="tpu_custom_call" | custom-call | tf_op jit(solution)/shard_map/pallas_call | solution.py:174

commit v2 on v1

--- a/solution.py
+++ b/solution.py
@@ -1,4 +1,3 @@
-import functools
 import math
 
 import jax
@@ -25,6 +24,7 @@
 LANES_FULL = 512
 PRODUCTS = COMPONENTS * COMPONENTS
 VALUES = PRODUCTS * PARTS
+WIDE = -(-8 * VALUES // 128) * 128
 
 EPSILON = 1e-06
 VMEM_LIMIT = 56 * 1024 * 1024
@@ -95,7 +95,53 @@
     return out.reshape(DEVICES, PARTS, LANES_FULL)
 
 
-def cross_kernel(slot_ref, spec_ref, out_ref, spec_full, planes, turned, placed):
+def route_kernel(slot_ref, order_ref, place_ref, shift_ref):
+    shape = (DEVICES, PER_OWNER)
+    tile = lax.broadcasted_iota(jnp.int32, shape, 0)
+    lane = lax.broadcasted_iota(jnp.int32, shape, 1)
+    slots = slot_ref[...]
+    shift = (slots // PER_OWNER - tile) & (DEVICES - 1)
+    slot = slots & (PER_OWNER - 1)
+    key = shift * PER_OWNER + lane
+
+    def count(i, total):
+        for k in range(8):
+            total = total + (pltpu.roll(key, i * 8 + k, 1) < key).astype(jnp.int32)
+        return total
+
+    rank = lax.fori_loop(0, PER_OWNER // 8, count, jnp.zeros(shape, jnp.int32))
+    packed = (rank << 21) | (shift << 14) | (lane << 7) | slot
+
+    def pick(i, found):
+        for k in range(8):
+            turned = pltpu.roll(packed, i * 8 + k, 1)
+            found = jnp.where((turned >> 21) == lane, turned, found)
+        return found
+
+    ordered = lax.fori_loop(0, PER_OWNER // 8, pick, jnp.zeros(shape, jnp.int32))
+    order_ref[...] = (ordered >> 7) & (PER_OWNER - 1)
+    shift = (ordered >> 14) & (DEVICES - 1)
+    shift_ref[...] = shift[:8]
+    slot = ordered & (PER_OWNER - 1)
+    for bit in range(7):
+        slot = jnp.where((shift >> bit) & 1 == 1, pltpu.roll(slot, 1 << bit, 0), slot)
+    place_ref[...] = slot
+
+
+def route(pair_slot):
+    tiles = pair_slot.reshape(8, 16, 8, 16).transpose(0, 3, 1, 2).reshape(DEVICES, PER_OWNER)
+    table = jax.ShapeDtypeStruct((DEVICES, PER_OWNER), jnp.int32)
+    return pl.pallas_call(
+        route_kernel,
+        out_shape=(table, table, jax.ShapeDtypeStruct((8, PER_OWNER), jnp.int32)),
+        in_specs=[pl.BlockSpec(memory_space=pltpu.VMEM)],
+        out_specs=[pl.BlockSpec(memory_space=pltpu.VMEM)] * 3,
+        compiler_params=pltpu.CompilerParams(vmem_limit_bytes=VMEM_LIMIT),
+        cost_estimate=pl.CostEstimate(flops=40_000_000, bytes_accessed=200_000, transcendentals=0),
+    )(tiles)
+
+
+def cross_kernel(order_ref, shift_ref, spec_ref, out_ref, spec_full, planes, columns, turned, moved):
     wide = spec_ref[...].astype(jnp.float32).reshape(STATIONS * PARTS, LANES_FULL)
     tiles = LANES_FULL // 128
     for t in range(tiles):
@@ -103,7 +149,13 @@
 
     def part(row):
         return jnp.concatenate(
-            [spec_full[t, pl.ds(row, STATIONS, stride=PARTS), :] for t in range(tiles)], axis=1
+            [
+                jnp.concatenate(
+                    [spec_full[t, pl.ds(low * PARTS + row, 8, stride=16 * PARTS), :] for low in range(16)], axis=0
+                )
+                for t in range(tiles)
+            ],
+            axis=1,
         )
 
     head = part(0)
@@ -132,67 +184,120 @@
                     row = (c * COMPONENTS + d) * PARTS + p * BINS + f
                     planes[pl.ds(row, STATIONS, stride=VALUES), :] = plane * scale
 
-    def place(a, carry):
-        turned[:, :VALUES] = planes[pl.ds(a * VALUES, VALUES), :].T
-        for b in range(STATIONS):
-            placed[pl.ds(slot_ref[a * STATIONS + b], 1), :] = turned[b : b + 1, :]
+    moves = [(shift_ref[...] >> bit) & 1 == 1 for bit in range(7)]
+
+    def rows_of(tile, cd):
+        return pl.ds(pl.multiple_of(tile * VALUES + cd * 8, 8), 8)
+
+    def first_turn(low, carry):
+        begin = pl.multiple_of(low * 8 * VALUES, 8)
+        for k in range(WIDE // 128):
+            count = min(128, 8 * VALUES - k * 128)
+            rows = planes[pl.ds(pl.multiple_of(begin + k * 128, 8), count), :]
+            columns[low, :, k * 128 : k * 128 + count] = rows.astype(jnp.bfloat16).T.astype(jnp.float32)
         return carry
 
-    lax.fori_loop(0, STATIONS, place, 0)
-
-    def finish(owner, carry):
-        out_ref[owner] = placed[pl.ds(owner * PER_OWNER, PER_OWNER), :].T[:VALUES].astype(jnp.bfloat16)
+    lax.fori_loop(0, 16, first_turn, 0, unroll=2)
+
+    pair = lax.broadcasted_iota(jnp.int32, (PER_OWNER, PER_OWNER), 0)
+
+    def second_turn(low, carry):
+        for k in range(WIDE // 128):
+            count = min(128, 8 * VALUES - k * 128)
+            block = columns[:, pl.ds(pl.multiple_of(low * 8, 8), 8), k * 128 : k * 128 + count]
+            turned[k * 128 : k * 128 + count, :] = block.reshape(PER_OWNER, count).T
+        for high in range(8):
+            tile = high * 16 + low
+            chosen = jnp.where(pair == order_ref[pl.ds(tile, 1), :], 1.0, 0.0).astype(jnp.bfloat16)
+            values = turned[high * VALUES : (high + 1) * VALUES, :].astype(jnp.bfloat16)
+            moved[pl.ds(pl.multiple_of(tile * VALUES, 8), VALUES), :] = jnp.dot(
+                values, chosen, preferred_element_type=jnp.float32
+            )
         return carry
 
-    lax.fori_loop(0, DEVICES, finish, 0)
-
-
-def cross(slots, spectra):
+    lax.fori_loop(0, 16, second_turn, 0)
+
+    def shift_eights(residue, carry):
+        for cd in range(PRODUCTS):
+            x = [moved[rows_of(residue + 8 * i, cd), :] for i in range(16)]
+            for bit in range(4):
+                x = [jnp.where(moves[3 + bit], x[(i - (1 << bit)) % 16], x[i]) for i in range(16)]
+            for i in range(16):
+                moved[rows_of(residue + 8 * i, cd), :] = x[i]
+        return carry
+
+    lax.fori_loop(0, 8, shift_eights, 0)
+
+    def finish(block, carry):
+        for cd in range(PRODUCTS):
+            x = [moved[rows_of((block * 16 + DEVICES - 7 + i) & (DEVICES - 1), cd), :] for i in range(23)]
+            for bit in range(3):
+                step = 1 << bit
+                x = [None] * step + [
+                    None if x[i - step] is None else jnp.where(moves[bit], x[i - step], x[i]) for i in range(step, 23)
+                ]
+            for i in range(16):
+                planes[rows_of(block * 16 + i, cd), :] = x[7 + i]
+        for i in range(16):
+            owner = block * 16 + i
+            out_ref[owner] = planes[pl.ds(pl.multiple_of(owner * VALUES, 8), VALUES), :].astype(jnp.bfloat16)
+        return carry
+
+    lax.fori_loop(0, 8, finish, 0)
+
+
+def cross(order, shift, spectra):
     return pl.pallas_call(
         cross_kernel,
         out_shape=jax.ShapeDtypeStruct((DEVICES, VALUES, PER_OWNER), jnp.bfloat16),
-        in_specs=[pl.BlockSpec(memory_space=pltpu.SMEM), pl.BlockSpec(memory_space=pltpu.VMEM)],
+        in_specs=[pl.BlockSpec(memory_space=pltpu.VMEM)] * 3,
         out_specs=pl.BlockSpec(memory_space=pltpu.VMEM),
         scratch_shapes=[
             pltpu.VMEM((LANES_FULL // 128, STATIONS * PARTS, 128), jnp.float32),
             pltpu.VMEM((STATIONS * VALUES, STATIONS), jnp.float32),
-            pltpu.VMEM((STATIONS, 128), jnp.float32),
-            pltpu.VMEM((DEVICES * PER_OWNER, 128), jnp.float32),
+            pltpu.VMEM((16, STATIONS, WIDE), jnp.float32),
+            pltpu.VMEM((8 * VALUES, STATIONS), jnp.float32),
+            pltpu.VMEM((STATIONS * VALUES, STATIONS), jnp.float32),
         ],
         compiler_params=pltpu.CompilerParams(vmem_limit_bytes=VMEM_LIMIT),
-    )(slots, spectra)
-
-
-def lag_kernel(cross_ref, table_ref, old_ref, out_ref):
-    row = pl.multiple_of(pl.program_id(0) * PARTS, PARTS)
-    spectra = cross_ref[:, pl.ds(row, PARTS), :].reshape(2 * FREQ_BINS, PER_OWNER)
-    lagged = lax.dot_general(spectra, table_ref[...], TN, preferred_element_type=jnp.float32)
-    out_ref[0] = old_ref[0] + lagged
-
-
-def lag(arrived, old_rows):
+    )(order, shift, spectra)
+
+
+def lag_kernel(owner_ref, cross_ref, table_ref, place_ref, old_ref, out_ref):
+    spectra = cross_ref[...].reshape(2 * FREQ_BINS, PER_OWNER)
+    row = lax.broadcasted_iota(jnp.int32, (PER_OWNER, PER_OWNER), 0)
+    chosen = jnp.where(row == place_ref[pl.ds(owner_ref[0], 1), :], 1.0, 0.0).astype(jnp.bfloat16)
+    rows = lax.dot_general(chosen, spectra, NT, preferred_element_type=jnp.float32).astype(jnp.bfloat16)
+    out_ref[0] = old_ref[0] + jnp.dot(rows, table_ref[...], preferred_element_type=jnp.float32)
+
+
+def lag(owner, arrived, place, old_rows):
     return pl.pallas_call(
         lag_kernel,
         grid=(PRODUCTS,),
         out_shape=jax.ShapeDtypeStruct((PRODUCTS, PER_OWNER, LAG_BINS), jnp.float32),
         in_specs=[
-            pl.BlockSpec((DEVICES, VALUES, PER_OWNER), lambda i: (0, 0, 0)),
+            pl.BlockSpec(memory_space=pltpu.SMEM),
+            pl.BlockSpec((DEVICES, PARTS, PER_OWNER), lambda i: (0, i, 0)),
             pl.BlockSpec((2 * FREQ_BINS, LAG_BINS), lambda i: (0, 0)),
+            pl.BlockSpec((DEVICES, PER_OWNER), lambda i: (0, 0)),
             pl.BlockSpec((1, PER_OWNER, LAG_BINS), lambda i: (i, 0, 0)),
         ],
         out_specs=pl.BlockSpec((1, PER_OWNER, LAG_BINS), lambda i: (i, 0, 0)),
         compiler_params=pltpu.CompilerParams(vmem_limit_bytes=VMEM_LIMIT),
-    )(arrived, jnp.asarray(lag_table()), old_rows)
+    )(owner, arrived, jnp.asarray(lag_table()), place, old_rows)
 
 
 def local(waveforms, availability, pair_slot, old_stack):
     axes = ("row", "col")
     spectra = whiten(waveforms.reshape(LANES, SAMPLES), availability)
     spectra = lax.all_to_all(spectra, axes, split_axis=0, concat_axis=0, tiled=True)
-    crossed = cross(pair_slot.reshape(-1), spectra)
+    order, place, shift = route(pair_slot)
+    crossed = cross(order, shift, spectra)
     arrived = lax.all_to_all(crossed, axes, split_axis=0, concat_axis=0, tiled=True)
     old_rows = jnp.transpose(old_stack, (1, 2, 0, 3)).reshape(PRODUCTS, PER_OWNER, LAG_BINS)
-    new_rows = lag(arrived, old_rows).reshape(COMPONENTS, COMPONENTS, PER_OWNER, LAG_BINS)
+    owner = (lax.axis_index("row") * lax.axis_size("col") + lax.axis_index("col")).astype(jnp.int32).reshape(1)
+    new_rows = lag(owner, arrived, place, old_rows).reshape(COMPONENTS, COMPONENTS, PER_OWNER, LAG_BINS)
     return jnp.transpose(new_rows, (2, 0, 1, 3))
 
 

time: 121 us -> 98.4 us (0.81)
  blocking collectives: 68.5 us -> 0 us
  waiting for transfers between devices: 0 us -> 42 us
  Pallas kernels: 52.4 us -> 36.3 us
  starting transfers between devices: 0 us -> 15.8 us
  local copies, waits for them, and re-layouts: 0 us -> 3.77 us
    all_to_all x2 -> x0, blocking collectives: 68.5 us -> none  [the longest x1 37.6 us: local(): lax.all_to_all(crossed, axes, split_axis=0, concat_axis=0, tiled=True)]
    all_to_all x0 -> x2, waiting for transfers between devices: none -> 42 us  [the longest x1 32.4 us: local(): lax.all_to_all(crossed, axes, split_axis=0, concat_axis=0, tiled=True)]
    pallas_call x1, Pallas kernels: 38.4 us -> 13.8 us  [cross(): pl.pallas_call(cross_kernel, out_shape=jax.ShapeDtypeStruct((DEVICES, VAL...]
    all_to_all x0 -> x2, starting transfers between devices: none -> 15.8 us  [the longest x1 11.5 us: local(): lax.all_to_all(spectra, axes, split_axis=0, concat_axis=0, tiled=True)]
    pallas_call x0 -> x1, Pallas kernels: none -> 8.24 us  [route(): pl.pallas_call(route_kernel, out_shape=(table, table, jax.ShapeDtypeStruc...]
    unnamed x0 -> x6, local copies, waits for them, and re-layouts: none -> 2.37 us
    reshape x0 -> x4, local copies, waits for them, and re-layouts: none -> 1.4 us  [route(): pair_slot.reshape(8, 16, 8, 16).transpose(0, 3, 1, 2)]
  transfers between devices with their start and end apart: 0 -> 2, of which waited for: 0 -> 2; matrix products, arithmetic and copies ran while one was open for 0% -> 1% of each run, Pallas kernels for 0% -> 8%
where the time goes in v2:
time: 98.4 us; the launch traced here: 97.9 us
  waiting for transfers between devices  42 us (43%)
  Pallas kernels  36.3 us (37%)
  starting transfers between devices  15.8 us (16%)
  local copies, waits for them, and re-layouts  3.77 us (4%)
    all_to_all x1, waiting for transfers between devices, local(): lax.all_to_all(crossed, axes, split_axis=0, concat_axis=0, tiled=True)  32.4 us
    pallas_call x1, Pallas kernels, cross(): pl.pallas_call(cross_kernel, out_shape=jax.ShapeDtypeStruct((DEVICES, VAL...  13.8 us
    all_to_all x1, starting transfers between devices, local(): lax.all_to_all(spectra, axes, split_axis=0, concat_axis=0, tiled=True)  11.5 us
    all_to_all x1, waiting for transfers between devices, local(): lax.all_to_all(spectra, axes, split_axis=0, concat_axis=0, tiled=True)  9.62 us
    pallas_call x1, Pallas kernels, lag(): pl.pallas_call(lag_kernel, grid=(PRODUCTS,), out_shape=jax.ShapeDtypeStru...  9.03 us
    pallas_call x1, Pallas kernels, route(): pl.pallas_call(route_kernel, out_shape=(table, table, jax.ShapeDtypeStruc...  8.24 us
    pallas_call x1, Pallas kernels, whiten(): pl.pallas_call(whiten_kernel, out_shape=jax.ShapeDtypeStruct((FREQ_BINS /...  5.28 us
    all_to_all x1, starting transfers between devices, local(): lax.all_to_all(crossed, axes, split_axis=0, concat_axis=0, tiled=True)  4.27 us
  transfers between devices with their start and end apart: 2, of which 2 were waited for; matrix products, arithmetic and copies ran while one was open for 1% of the time, Pallas kernels for 8%

profile of v2, /device:TPU:1, one launch (start us, length us, event | category | flops | bytes accessed | tf_op | source)
XLA Modules:
  0.0 97.9 jit_solution(3723492263025795898)
XLA Ops:
  0.0 0.0 copy-start.2
  0.0 5.3 %shard_map.83 = bf16[64,2,8,512]{3,2,1,0:T(8,128)(2,1)} custom-call(s32[1,2]{1,0:T(1,128)} %avail_ref.1, bf16[480,1024]{1,0:T(8,128)(2,1)} %bitcast.19, bf16[1024,1024]{1,0:T(8,128)(2,1)} %constant.19.clone.dft_ref, bf16[512,512]{1,0:T(8,128)(2,1)} %constant.20.clone.band_ref, f32[512,1]{1,0:T(8,128)} %constant.21.clone.share_ref), custom_call_target="tpu_custom_call" | custom-call | tf_op jit(solution)/shard_map/pallas_call | solution.py:87
  5.3 11.5 %all-to-all-start = ((bf16[128,8,512]{2,1,0:T(8,128)(2,1)}), bf16[128,8,512]{2,1,0:T(8,128)(2,1)S(1)}, u32[]{:S(2)}, u32[]{:S(2)}) async-start(bf16[128,8,512]{2,1,0:T(8,128)(2,1)} %bitcast.16), calls=%async_computation | async-start | bytes 2097152 | tf_op jit(solution)/shard_map/all_to_all | solution.py:294
  16.8 0.0 copy-done.2
  16.8 0.2 reshape.22
  17.0 0.3 copy.13
  17.3 0.2 reshape.23
  17.5 0.7 copy.11.slot_ref
  18.2 8.2 %shard_map.82 = (s32[128,128]{1,0:T(8,128)}, s32[128,128]{1,0:T(8,128)}, s32[8,128]{1,0:T(8,128)}) custom-call(s32[128,128]{1,0:T(8,128)} %copy.11.slot_ref), custom_call_target="tpu_custom_call" | custom-call | flops 40000000 | bytes 200000 | tf_op jit(solution)/shard_map/pallas_call | solution.py:134
  26.5 9.6 %all-to-all-done.spec_ref = bf16[128,8,512]{2,1,0:T(8,128)(2,1)S(1)} async-done(((bf16[128,8,512]{2,1,0:T(8,128)(2,1)}), bf16[128,8,512]{2,1,0:T(8,128)(2,1)S(1)}, u32[]{:S(2)}, u32[]{:S(2)}) %all-to-all-start) | async-done | bytes 1048608 | tf_op jit(solution)/shard_map/all_to_all | solution.py:294
  36.1 0.0 copy-start.1
  36.1 1.0 copy-done.1
  37.0 13.8 %shard_map.84 = bf16[128,72,128]{2,1,0:T(8,128)(2,1)} custom-call(s32[128,128]{1,0:T(8,128)} %get-tuple-element.8.order_ref, s32[8,128]{1,0:T(8,128)} %get-tuple-element.9.shift_ref, bf16[128,8,512]{2,1,0:T(8,128)(2,1)} %copy-done.1), custom_call_target="tpu_custom_call" | custom-call | tf_op jit(solution)/shard_map/pallas_call | solution.py:250
  50.8 4.3 %all-to-all-start.1 = ((bf16[128,72,128]{2,1,0:T(8,128)(2,1)}), bf16[128,72,128]{2,1,0:T(8,128)(2,1)S(1)}, u32[]{:S(2)}, u32[]{:S(2)}) async-start(bf16[128,72,128]{2,1,0:T(8,128)(2,1)} %shard_map.84), calls=%async_computation.1 | async-start | bytes 4718592 | tf_op jit(solution)/shard_map/all_to_all | solution.py:297
  55.1 32.4 %all-to-all-done.1.cross_ref = bf16[128,72,128]{2,1,0:T(8,128)(2,1)S(1)} async-done(((bf16[128,72,128]{2,1,0:T(8,128)(2,1)}), bf16[128,72,128]{2,1,0:T(8,128)(2,1)S(1)}, u32[]{:S(2)}, u32[]{:S(2)}) %all-to-all-start.1) | async-done | bytes 2359328 | tf_op jit(solution)/shard_map/all_to_all | solution.py:297
  87.5 0.0 copy-start
  87.5 1.4 %copy-done = bf16[128,72,128]{2,1,0:T(8,128)(2,1)} copy-done((bf16[128,72,128]{2,1,0:T(8,128)(2,1)}, bf16[128,72,128]{2,1,0:T(8,128)(2,1)S(1)}, u32[]{:S(2)}) %copy-start) | copy-done | bytes 2359320
  88.9 9.0 %shard_map.85 = f32[9,128,512]{2,1,0:T(8,128)} custom-call(s32[1]{0:T(128)} %bitcast.owner_ref, bf16[128,72,128]{2,1,0:T(8,128)(2,1)} %copy-done, bf16[1024,512]{1,0:T(8,128)(2,1)} %constant.22.clone.table_ref, s32[128,128]{1,0:T(8,128)} %get-tuple-element.10.place_ref, f32[9,128,512]{2,1,0:T(8,128)} %bitcast.17), custom_call_target="tpu_custom_call" | custom-call | tf_op jit(solution)/shard_map/pallas_call | solution.py:275
Async XLA Ops:
  0.0 16.8 %copy-start.2 = (s32[128,128]{1,0:T(8,128)S(1)}, s32[128,128]{1,0:T(8,128)}, u32[]{:S(2)}) copy-start(s32[128,128]{1,0:T(8,128)} %param.10) | copy-start | bytes 196612
  5.3 30.8 %all-to-all-start = ((bf16[128,8,512]{2,1,0:T(8,128)(2,1)}), bf16[128,8,512]{2,1,0:T(8,128)(2,1)S(1)}, u32[]{:S(2)}, u32[]{:S(2)}) async-start(bf16[128,8,512]{2,1,0:T(8,128)(2,1)} %bitcast.16), calls=%async_computation | async-start | bytes 2097152 | tf_op jit(solution)/shard_map/all_to_all | solution.py:294
  36.1 1.0 copy-start.1
  50.8 36.6 %all-to-all-start.1 = ((bf16[128,72,128]{2,1,0:T(8,128)(2,1)}), bf16[128,72,128]{2,1,0:T(8,128)(2,1)S(1)}, u32[]{:S(2)}, u32[]{:S(2)}) async-start(bf16[128,72,128]{2,1,0:T(8,128)(2,1)} %shard_map.84), calls=%async_computation.1 | async-start | bytes 4718592 | tf_op jit(solution)/shard_map/all_to_all | solution.py:297
  87.5 1.4 %copy-start = (bf16[128,72,128]{2,1,0:T(8,128)(2,1)}, bf16[128,72,128]{2,1,0:T(8,128)(2,1)S(1)}, u32[]{:S(2)}) copy-start(bf16[128,72,128]{2,1,0:T(8,128)(2,1)S(1)} %all-to-all-done.1.cross_ref) | copy-start | bytes 7077892

commit v3 on v2

v3 whole, which is shorter than its diff:
```python
import math

import jax
import jax.numpy as jnp
import ml_dtypes
import numpy as np
from jax import lax
from jax.experimental import pallas as pl
from jax.experimental.pallas import tpu as pltpu
from jax.sharding import PartitionSpec as P

SEGMENTS = 160
COMPONENTS = 3
SAMPLES = 1024
LAG_BINS = 512
BAND_HALF = 64
FREQ_BINS = 512
DEVICES = 128
STATIONS = 128
PER_OWNER = 128
BINS = FREQ_BINS // DEVICES
PARTS = 2 * BINS
LANES = COMPONENTS * SEGMENTS
LANES_FULL = 512
PRODUCTS = COMPONENTS * COMPONENTS
VALUES = PRODUCTS * PARTS
ROWS = -(-VALUES // 16) * 16
APART = ROWS + 8
WIDE = 8 * ROWS

LEAVE = 32

EPSILON = 1e-06
MIB = 1024 * 1024
NT = (((1,), (1,)), ((), ()))
TN = (((0,), (0,)), ((), ()))


def dft_table():
    turns = np.arange(FREQ_BINS)[:, None] * np.arange(SAMPLES)[None, :] % SAMPLES
    turns = turns.astype(np.float32) * np.float32(2.0 * math.pi / SAMPLES)
    table = np.concatenate([np.cos(turns), -np.sin(turns)], axis=0)
    return table.astype(ml_dtypes.bfloat16)


def band_table():
    bin_ids = np.arange(FREQ_BINS)
    return (np.abs(bin_ids[:, None] - bin_ids[None, :]) <= BAND_HALF).astype(ml_dtypes.bfloat16)


def lag_table():
    bin_ids = np.arange(FREQ_BINS)
    lag_ids = np.arange(LAG_BINS) - LAG_BINS // 2
    turns = bin_ids[:, None] * lag_ids[None, :] % SAMPLES
    turns = turns.astype(np.float32) * np.float32(2.0 * math.pi / SAMPLES)
    weight = np.where(bin_ids == 0, 1.0, 2.0).astype(np.float32)[:, None] / np.float32(math.sqrt(FREQ_BINS))
    both = np.stack([weight * np.cos(turns), -weight * np.sin(turns)])
    return both.transpose(1, 0, 2).reshape(2 * FREQ_BINS, LAG_BINS).astype(ml_dtypes.bfloat16)


def lane_runs():
    whole = [(c * SEGMENTS, c * 128, 128) for c in range(COMPONENTS)]
    rest = SEGMENTS - 128
    return whole + [(c * SEGMENTS + 128, COMPONENTS * 128 + c * rest, rest) for c in range(COMPONENTS)]


def whiten_kernel(
    avail_hbm, wave_hbm, dft_hbm, band_hbm, out_ref, avail, wave, dft, band, mixed, avail_sem, wave_sems, dft_sems, band_sem
):
    runs = lane_runs()
    wave_copies = [
        pltpu.make_async_copy(wave_hbm.at[pl.ds(row, count)], wave.at[pl.ds(begin, count)], wave_sems.at[i])
        for i, (row, begin, count) in enumerate(runs)
    ]
    dft_copies = [
        pltpu.make_async_copy(
            dft_hbm.at[pl.ds(i * FREQ_BINS, FREQ_BINS)], dft.at[pl.ds(i * FREQ_BINS, FREQ_BINS)], dft_sems.at[i]
        )
        for i in range(2)
    ]
    band_copy = pltpu.make_async_copy(band_hbm, band, band_sem)
    avail_copy = pltpu.make_async_copy(avail_hbm, avail, avail_sem)
    for copy in wave_copies + dft_copies + [band_copy, avail_copy]:
        copy.start()
    wave[LANES:] = jnp.zeros((LANES_FULL - LANES, SAMPLES), jnp.bfloat16)
    for copy in wave_copies:
        copy.wait()
    waves = wave[...].T
    dft_copies[0].wait()
    real = jnp.dot(dft[:FREQ_BINS], waves, preferred_element_type=jnp.float32)
    dft_copies[1].wait()
    imag = jnp.dot(dft[FREQ_BINS:], waves, preferred_element_type=jnp.float32)
    power = real * real + imag * imag
    high = power.astype(jnp.bfloat16)
    low = (power - high.astype(jnp.float32)).astype(jnp.bfloat16)
    band_copy.wait()
    near = band[...]
    smooth = jnp.dot(near, high, preferred_element_type=jnp.float32) + jnp.dot(
        near, low, preferred_element_type=jnp.float32
    )
    bin_id = lax.broadcasted_iota(jnp.int32, (FREQ_BINS, 1), 0)
    width = jnp.minimum(bin_id, BAND_HALF) + jnp.minimum(FREQ_BINS - 1 - bin_id, BAND_HALF) + 1
    lane = lax.broadcasted_iota(jnp.int32, (1, LANES_FULL), 1)
    segment = jnp.where(lane < COMPONENTS * 128, lane & 127, 128 + (lane & (SEGMENTS - 129)))
    avail_copy.wait()
    first, last = avail[0, 0], avail[0, 1]
    mask = ((segment >= first) & (segment < last) & (lane < LANES)).astype(jnp.float32)
    factor = lax.rsqrt(smooth * (1.0 / width.astype(jnp.float32)) + EPSILON) * mask
    spare = jnp.where(lane == LANES, first, jnp.where(lane == LANES + 1, last, 0)).astype(jnp.float32)
    real = real * factor + spare
    imag = imag * factor + spare
    for t in range(LANES_FULL // 128):
        mixed[t, pl.ds(0, FREQ_BINS, stride=2), :] = real[:, t * 128 : (t + 1) * 128]
        mixed[t, pl.ds(1, FREQ_BINS, stride=2), :] = imag[:, t * 128 : (t + 1) * 128]
    for t in range(LANES_FULL // 128):
        out_ref[:, :, t * 128 : (t + 1) * 128] = mixed[t].astype(jnp.bfloat16).reshape(DEVICES, PARTS, 128)


def whiten(waves, availability):
    in_hbm = (availability, waves, jnp.asarray(dft_table()), jnp.asarray(band_table()))
    return pl.pallas_call(
        whiten_kernel,
        out_shape=jax.ShapeDtypeStruct((DEVICES, PARTS, LANES_FULL), jnp.bfloat16),
        in_specs=[pl.BlockSpec(memory_space=pltpu.HBM)] * 4,
        out_specs=pl.BlockSpec(memory_space=pltpu.VMEM),
        scratch_shapes=[
            pltpu.SMEM((1, 2), jnp.int32),
            pltpu.VMEM((LANES_FULL, SAMPLES), jnp.bfloat16),
            pltpu.VMEM((2 * FREQ_BINS, SAMPLES), jnp.bfloat16),
            pltpu.VMEM((FREQ_BINS, FREQ_BINS), jnp.bfloat16),
            pltpu.VMEM((LANES_FULL // 128, 2 * FREQ_BINS, 128), jnp.float32),
            pltpu.SemaphoreType.DMA,
            pltpu.SemaphoreType.DMA((2 * COMPONENTS,)),
            pltpu.SemaphoreType.DMA((2,)),
            pltpu.SemaphoreType.DMA,
        ],
        compiler_params=pltpu.CompilerParams(vmem_limit_bytes=20 * MIB),
    )(*(pltpu.with_memory_space_constraint(x, pltpu.HBM) for x in in_hbm))


def route_kernel(slot_ref, order_ref, place_ref, shift_ref):
    shape = (DEVICES, PER_OWNER)
    tile = lax.broadcasted_iota(jnp.int32, shape, 0)
    lane = lax.broadcasted_iota(jnp.int32, shape, 1)
    slots = slot_ref[...]
    shift = (slots // PER_OWNER - tile) & (DEVICES - 1)
    slot = slots & (PER_OWNER - 1)
    key = shift * PER_OWNER + lane

    def count(i, total):
        for k in range(8):
            total = total + (pltpu.roll(key, i * 8 + k, 1) < key).astype(jnp.int32)
        return total

    rank = lax.fori_loop(0, PER_OWNER // 8, count, jnp.zeros(shape, jnp.int32))
    packed = (rank << 21) | (shift << 14) | (lane << 7) | slot

    def pick(i, found):
        for k in range(8):
            turned = pltpu.roll(packed, i * 8 + k, 1)
            found = jnp.where((turned >> 21) == lane, turned, found)
        return found

    ordered = lax.fori_loop(0, PER_OWNER // 8, pick, jnp.zeros(shape, jnp.int32))
    order_ref[...] = (ordered >> 7) & (PER_OWNER - 1)
    shift = (ordered >> 14) & (DEVICES - 1)
    shift_ref[...] = shift[:8]
    slot = ordered & (PER_OWNER - 1)
    for bit in range(7):
        slot = jnp.where((shift >> bit) & 1 == 1, pltpu.roll(slot, 1 << bit, 0), slot)
    place_ref[...] = slot


def route(pair_slot):
    tiles = pair_slot.reshape(8, 16, 8, 16).transpose(0, 3, 1, 2).reshape(DEVICES, PER_OWNER)
    table = jax.ShapeDtypeStruct((DEVICES, PER_OWNER), jnp.int32)
    return pl.pallas_call(
        route_kernel,
        out_shape=(table, table, jax.ShapeDtypeStruct((8, PER_OWNER), jnp.int32)),
        in_specs=[pl.BlockSpec(memory_space=pltpu.VMEM)],
        out_specs=[pl.BlockSpec(memory_space=pltpu.VMEM)] * 3,
        compiler_params=pltpu.CompilerParams(vmem_limit_bytes=4 * MIB),
        cost_estimate=pl.CostEstimate(flops=40_000_000, bytes_accessed=200_000, transcendentals=0),
    )(tiles)


def cross_kernel(
    order_ref, shift_ref, spec_ref, out_hbm, spec_full, planes, columns, turned, placed, moved, ready, out_sems
):
    wide = spec_ref[...].astype(jnp.float32).reshape(STATIONS * PARTS, LANES_FULL)
    tiles = LANES_FULL // 128
    for t in range(tiles):
        spec_full[t] = wide[:, t * 128 : (t + 1) * 128]

    def part(row, t):
        return jnp.concatenate(
            [spec_full[t, pl.ds(low * PARTS + row, 8, stride=16 * PARTS), :] for low in range(16)], axis=0
        )

    head = part(0, LANES // 128)
    spare = LANES % 128
    first = jnp.broadcast_to(head[:, spare : spare + 1], (STATIONS, STATIONS))
    last = jnp.broadcast_to(head[:, spare + 1 : spare + 2], (STATIONS, STATIONS))
    counts = jnp.minimum(last, last.T) - jnp.maximum(first, first.T)
    one = lax.broadcasted_iota(jnp.int32, (STATIONS, STATIONS), 0)
    two = lax.broadcasted_iota(jnp.int32, (STATIONS, STATIONS), 1)
    scale = jnp.where(one == two, 0.0, 1.0 / counts)

    def fold(row):
        pieces = [part(row, t).astype(jnp.bfloat16) for t in range(tiles)]
        rest = SEGMENTS - 128
        return jnp.concatenate(
            [
                jnp.concatenate([pieces[c], pieces[-1][:, c * rest : (c + 1) * rest]], axis=1)
                for c in range(COMPONENTS)
            ],
            axis=0,
        )

    def product(x, y):
        return jnp.dot(x, y, preferred_element_type=jnp.float32)

    for f in range(BINS):
        real, imag = fold(2 * f), fold(2 * f + 1)
        real_t, imag_t = real.T, imag.T
        both = (product(real, real_t) + product(imag, imag_t), product(imag, real_t) - product(real, imag_t))
        for p in range(2):
            for c in range(COMPONENTS):
                for d in range(COMPONENTS):
                    plane = both[p][c * STATIONS : (c + 1) * STATIONS, d * STATIONS : (d + 1) * STATIONS]
                    row = (c * COMPONENTS + d) * PARTS + 2 * f + p
                    planes[pl.ds(row, STATIONS, stride=APART), :] = plane * scale

    moves = [(shift_ref[...] >> bit) & 1 == 1 for bit in range(7)]

    def first_turn(i, carry):
        two = 16 * APART
        source = planes.at[pl.ds(pl.multiple_of(i * two, 8), two)]
        target = columns.at[:, pl.ds(pl.multiple_of(i * 16, 16), 16)]
        for k in range(WIDE // 128):
            sides = []
            for side in range(2):
                rows = []
                for begin in range(k * 128, (k + 1) * 128, 8):
                    high, value = divmod(begin, ROWS)
                    row = (side * 8 + high) * APART + value
                    rows.append(source[row : row + 8, :])
                rows = jnp.concatenate(rows, axis=0).astype(jnp.bfloat16).T
                sides.append(rows.astype(jnp.float32).reshape(16, 8, 128))
            target[:, :, k * 128 : (k + 1) * 128] = jnp.concatenate(sides, axis=1).astype(jnp.bfloat16)
        return carry

    lax.fori_loop(0, 8, first_turn, 0, unroll=2)

    pair = lax.broadcasted_iota(jnp.int32, (PER_OWNER, PER_OWNER), 0)

    def second_turn(i, carry):
        source = columns.at[pl.ds(2 * i, 2)]
        for side in range(2):
            for k in range(WIDE // 128):
                turned[side, k * 128 : (k + 1) * 128, :] = source[side, :, k * 128 : (k + 1) * 128].T
        targets = [moved.at[pl.ds(high * 16 + 2 * i, 2)] for high in range(9)]
        for side in range(2):
            for high in range(8):
                order = order_ref[pl.ds(high * 16 + 2 * i + side, 1), :]
                chosen = jnp.where(pair == order, 1.0, 0.0).astype(jnp.bfloat16)
                values = turned[side, high * ROWS : (high + 1) * ROWS, :]
                placed[side, high * ROWS : (high + 1) * ROWS, :] = jnp.dot(
                    values, chosen, preferred_element_type=jnp.float32
                )
            for group in range(0, VALUES, 8):
                x = [placed[side, high * ROWS + group : high * ROWS + group + 8, :] for high in range(8)]
                for bit in range(3):
                    x = [jnp.where(moves[4 + bit], x[(high - (1 << bit)) % 8], x[high]) for high in range(8)]
                for high in range(9):
                    targets[high][side, group : group + 8, :] = x[(high - 1) % 8]
        return carry

    lax.fori_loop(0, 8, second_turn, 0)

    def leave(block):
        some = pl.ds(pl.multiple_of(block * LEAVE, LEAVE), LEAVE)
        return pltpu.make_async_copy(ready.at[some], out_hbm.at[some], out_sems.at[block])

    def finish(block, carry):
        source = moved.at[pl.ds(block * LEAVE + 1, LEAVE + 15)]
        target = ready.at[pl.ds(block * LEAVE, LEAVE)]
        for group in range(0, VALUES, 8):
            x = [source[i, group : group + 8, :] for i in range(LEAVE + 15)]
            for bit in reversed(range(4)):
                step = 1 << bit
                x = [jnp.where(moves[bit], x[i - step], x[i]) for i in range(step, len(x))]
            for i in range(LEAVE):
                target[i, group : group + 8, :] = x[i].astype(jnp.bfloat16)
        leave(block).start()
        return carry

    lax.fori_loop(0, DEVICES // LEAVE, finish, 0)
    for block in range(DEVICES // LEAVE):
        leave(block).wait()


def cross(order, shift, spectra):
    return pl.pallas_call(
        cross_kernel,
        out_shape=jax.ShapeDtypeStruct((DEVICES, VALUES, PER_OWNER), jnp.bfloat16),
        in_specs=[pl.BlockSpec(memory_space=pltpu.VMEM)] * 3,
        out_specs=pl.BlockSpec(memory_space=pltpu.HBM),
        scratch_shapes=[
            pltpu.VMEM((LANES_FULL // 128, STATIONS * PARTS, 128), jnp.float32),
            pltpu.VMEM((STATIONS * APART, STATIONS), jnp.float32),
            pltpu.VMEM((16, STATIONS, WIDE), jnp.bfloat16),
            pltpu.VMEM((2, WIDE, STATIONS), jnp.bfloat16),
            pltpu.VMEM((2, WIDE, STATIONS), jnp.float32),
            pltpu.VMEM((DEVICES + 16, VALUES, PER_OWNER), jnp.float32),
            pltpu.VMEM((DEVICES, VALUES, PER_OWNER), jnp.bfloat16),
            pltpu.SemaphoreType.DMA((DEVICES // LEAVE,)),
        ],
        compiler_params=pltpu.CompilerParams(vmem_limit_bytes=28 * MIB),
    )(order, shift, spectra)


def lag_kernel(owner_ref, cross_ref, table_ref, place_ref, old_hbm, out_hbm, old, new, old_sems, new_sems):
    old_copies = [pltpu.make_async_copy(old_hbm.at[c], old.at[c], old_sems.at[c]) for c in range(COMPONENTS)]
    new_copies = [pltpu.make_async_copy(new.at[c], out_hbm.at[c], new_sems.at[c]) for c in range(COMPONENTS)]
    for copy in old_copies:
        copy.start()
    row = lax.broadcasted_iota(jnp.int32, (PER_OWNER, PER_OWNER), 0)
    chosen = jnp.where(row == place_ref[pl.ds(owner_ref[0], 1), :], 1.0, 0.0).astype(jnp.bfloat16)
    for c in range(COMPONENTS):
        rows = []
        for cd in range(c * COMPONENTS, (c + 1) * COMPONENTS):
            spectra = cross_ref[:, cd * PARTS : (cd + 1) * PARTS, :].reshape(2 * FREQ_BINS, PER_OWNER)
            turned = lax.dot_general(chosen, spectra, NT, preferred_element_type=jnp.float32)
            rows.append(turned.astype(jnp.bfloat16))
        lagged = jnp.dot(jnp.concatenate(rows, axis=0), table_ref[...], preferred_element_type=jnp.float32)
        old_copies[c].wait()
        new[c] = old[c] + lagged.reshape(COMPONENTS, PER_OWNER, LAG_BINS)
        new_copies[c].start()
    for copy in new_copies:
        copy.wait()


def lag(owner, arrived, place, old_rows):
    shape = (COMPONENTS, COMPONENTS, PER_OWNER, LAG_BINS)
    return pl.pallas_call(
        lag_kernel,
        out_shape=jax.ShapeDtypeStruct(shape, jnp.float32),
        in_specs=[pl.BlockSpec(memory_space=pltpu.SMEM)]
        + [pl.BlockSpec(memory_space=pltpu.VMEM)] * 3
        + [pl.BlockSpec(memory_space=pltpu.HBM)],
        out_specs=pl.BlockSpec(memory_space=pltpu.HBM),
        scratch_shapes=[
            pltpu.VMEM(shape, jnp.float32),
            pltpu.VMEM(shape, jnp.float32),
            pltpu.SemaphoreType.DMA((COMPONENTS,)),
            pltpu.SemaphoreType.DMA((COMPONENTS,)),
        ],
        compiler_params=pltpu.CompilerParams(vmem_limit_bytes=24 * MIB),
    )(owner, arrived, jnp.asarray(lag_table()), place, pltpu.with_memory_space_constraint(old_rows, pltpu.HBM))


def local(waveforms, availability, pair_slot, old_stack):
    axes = ("row", "col")
    spectra = whiten(waveforms.reshape(LANES, SAMPLES), availability)
    spectra = lax.all_to_all(spectra, axes, split_axis=0, concat_axis=0, tiled=True)
    order, place, shift = route(pair_slot)
    crossed = cross(order, shift, spectra)
    arrived = lax.all_to_all(crossed, axes, split_axis=0, concat_axis=0, tiled=True)
    old_rows = jnp.transpose(old_stack, (1, 2, 0, 3))
    owner = (lax.axis_index("row") * lax.axis_size("col") + lax.axis_index("col")).astype(jnp.int32).reshape(1)
    return jnp.transpose(lag(owner, arrived, place, old_rows), (2, 0, 1, 3))


def solution(mesh):
    return jax.shard_map(
        local,
        mesh=mesh,
        in_specs=(
            P(("row", "col"), None, None, None),
            P(("row", "col"), None),
            P(),
            P(("row", "col"), None, None, None),
        ),
        out_specs=P(("row", "col"), None, None, None),
        check_vma=False,
    )
```

time: 98.4 us -> 87.3 us (0.89)
  Pallas kernels: 36.3 us -> 26.2 us
  local copies, waits for them, and re-layouts: 3.77 us -> 0.78 us
  waiting for transfers between devices: 42 us -> 44.1 us
    pallas_call x2, Pallas kernels: 14.3 us -> 9.4 us  [the longest x1 5.48 us: whiten(): pl.pallas_call(whiten_kernel, out_shape=jax.ShapeDtypeStruct((DEVICES, PA...]
    pallas_call x1, Pallas kernels: 13.8 us -> 9.99 us  [cross(): pl.pallas_call(cross_kernel, out_shape=jax.ShapeDtypeStruct((DEVICES, VAL...]
    unnamed x6 -> x4, local copies, waits for them, and re-layouts: 2.37 us -> 0.01 us
    all_to_all x1, waiting for transfers between devices: 9.62 us -> 11.7 us  [local(): lax.all_to_all(spectra, axes, split_axis=0, concat_axis=0, tiled=True)]
    pallas_call x1, Pallas kernels: 8.24 us -> 6.77 us  [route(): pl.pallas_call(route_kernel, out_shape=(table, table, jax.ShapeDtypeStruc...]
where the time goes in v3:
time: 87.3 us; the launch traced here: 87 us
  waiting for transfers between devices  44.1 us (51%)
  Pallas kernels  26.2 us (30%)
  starting transfers between devices  15.9 us (18%)
    all_to_all x1, waiting for transfers between devices, local(): lax.all_to_all(crossed, axes, split_axis=0, concat_axis=0, tiled=True)  32.4 us
    all_to_all x1, waiting for transfers between devices, local(): lax.all_to_all(spectra, axes, split_axis=0, concat_axis=0, tiled=True)  11.7 us
    all_to_all x1, starting transfers between devices, local(): lax.all_to_all(spectra, axes, split_axis=0, concat_axis=0, tiled=True)  11.5 us
    pallas_call x1, Pallas kernels, cross(): pl.pallas_call(cross_kernel, out_shape=jax.ShapeDtypeStruct((DEVICES, VAL...  9.99 us
    pallas_call x1, Pallas kernels, route(): pl.pallas_call(route_kernel, out_shape=(table, table, jax.ShapeDtypeStruc...  6.77 us
    pallas_call x1, Pallas kernels, whiten(): pl.pallas_call(whiten_kernel, out_shape=jax.ShapeDtypeStruct((DEVICES, PA...  5.48 us
    all_to_all x1, starting transfers between devices, local(): lax.all_to_all(crossed, axes, split_axis=0, concat_axis=0, tiled=True)  4.42 us
    pallas_call x1, Pallas kernels, lag(): pl.pallas_call(lag_kernel, out_shape=jax.ShapeDtypeStruct(shape, jnp.floa...  3.92 us
  transfers between devices with their start and end apart: 2, of which 2 were waited for; matrix products, arithmetic and copies ran while one was open for 1% of the time, Pallas kernels for 8%

profile of v3, /device:TPU:1, one launch (start us, length us, event | category | flops | bytes accessed | tf_op | source)
XLA Modules:
  0.0 87.0 jit_solution(8083745641854606013)
XLA Ops:
  0.0 0.0 copy-start.1
  0.0 5.5 %shard_map.74 = bf16[128,8,512]{2,1,0:T(8,128)(2,1)} custom-call(s32[1,2]{1,0:T(1,128)} %avail_hbm.1, bf16[480,1024]{1,0:T(8,128)(2,1)} %bitcast.13, bf16[1024,1024]{1,0:T(8,128)(2,1)} %constant.17.clone.dft_hbm, bf16[512,512]{1,0:T(8,128)(2,1)} %constant.18.clone.band_hbm), custom_call_target="tpu_custom_call" | custom-call | tf_op jit(solution)/shard_map/pallas_call | solution.py:121
  5.5 11.5 %all-to-all-start = ((bf16[128,8,512]{2,1,0:T(8,128)(2,1)}), bf16[128,8,512]{2,1,0:T(8,128)(2,1)S(1)}, u32[]{:S(2)}, u32[]{:S(2)}) async-start(bf16[128,8,512]{2,1,0:T(8,128)(2,1)} %shard_map.74), calls=%async_computation | async-start | bytes 2097152 | tf_op jit(solution)/shard_map/all_to_all | solution.py:366
  17.0 0.0 copy-done.1
  17.0 0.2 reshape.13
  17.2 0.3 copy.12
  17.5 0.2 reshape.14
  17.7 0.1 copy.10.slot_ref
  17.8 6.8 %shard_map.73 = (s32[128,128]{1,0:T(8,128)S(1)}, s32[128,128]{1,0:T(8,128)S(1)}, s32[8,128]{1,0:T(8,128)S(1)}) custom-call(s32[128,128]{1,0:T(8,128)S(1)} %copy.10.slot_ref), custom_call_target="tpu_custom_call" | custom-call | flops 40000000 | bytes 200000 | tf_op jit(solution)/shard_map/pallas_call | solution.py:177
  24.6 11.7 %all-to-all-done.spec_ref = bf16[128,8,512]{2,1,0:T(8,128)(2,1)S(1)} async-done(((bf16[128,8,512]{2,1,0:T(8,128)(2,1)}), bf16[128,8,512]{2,1,0:T(8,128)(2,1)S(1)}, u32[]{:S(2)}, u32[]{:S(2)}) %all-to-all-start) | async-done | bytes 1048608 | tf_op jit(solution)/shard_map/all_to_all | solution.py:366
  36.3 10.0 %shard_map.75 = bf16[128,72,128]{2,1,0:T(8,128)(2,1)} custom-call(s32[128,128]{1,0:T(8,128)S(1)} %get-tuple-element.8.order_ref, s32[8,128]{1,0:T(8,128)S(1)} %get-tuple-element.9.shift_ref, bf16[128,8,512]{2,1,0:T(8,128)(2,1)S(1)} %all-to-all-done.spec_ref), custom_call_target="tpu_custom_call" | custom-call | tf_op jit(solution)/shard_map/pallas_call | solution.py:304
  46.3 0.0 copy-start
  46.3 4.4 %all-to-all-start.1 = ((bf16[128,72,128]{2,1,0:T(8,128)(2,1)}), bf16[128,72,128]{2,1,0:T(8,128)(2,1)S(1)}, u32[]{:S(2)}, u32[]{:S(2)}) async-start(bf16[128,72,128]{2,1,0:T(8,128)(2,1)} %shard_map.75), calls=%async_computation.1 | async-start | bytes 4718592 | tf_op jit(solution)/shard_map/all_to_all | solution.py:369
  50.7 32.4 %all-to-all-done.1.cross_ref = bf16[128,72,128]{2,1,0:T(8,128)(2,1)S(1)} async-done(((bf16[128,72,128]{2,1,0:T(8,128)(2,1)}), bf16[128,72,128]{2,1,0:T(8,128)(2,1)S(1)}, u32[]{:S(2)}, u32[]{:S(2)}) %all-to-all-start.1) | async-done | bytes 2359328 | tf_op jit(solution)/shard_map/all_to_all | solution.py:369
  83.1 0.0 copy-done
  83.1 3.9 %shard_map.76 = f32[3,3,128,512]{3,2,1,0:T(8,128)} custom-call(s32[1]{0:T(128)} %bitcast.owner_ref, bf16[128,72,128]{2,1,0:T(8,128)(2,1)S(1)} %all-to-all-done.1.cross_ref, bf16[1024,512]{1,0:T(8,128)(2,1)S(1)} %copy-done, s32[128,128]{1,0:T(8,128)S(1)} %get-tuple-element.10.place_ref, f32[3,3,128,512]{3,2,1,0:T(8,128)} %bitcast.11), custom_call_target="tpu_custom_call" | custom-call | tf_op jit(solution)/shard_map/pallas_call | solution.py:346
Async XLA Ops:
  0.0 17.0 %copy-start.1 = (s32[128,128]{1,0:T(8,128)S(1)}, s32[128,128]{1,0:T(8,128)}, u32[]{:S(2)}) copy-start(s32[128,128]{1,0:T(8,128)} %param.9) | copy-start | bytes 196612
  5.5 30.8 %all-to-all-start = ((bf16[128,8,512]{2,1,0:T(8,128)(2,1)}), bf16[128,8,512]{2,1,0:T(8,128)(2,1)S(1)}, u32[]{:S(2)}, u32[]{:S(2)}) async-start(bf16[128,8,512]{2,1,0:T(8,128)(2,1)} %shard_map.74), calls=%async_computation | async-start | bytes 2097152 | tf_op jit(solution)/shard_map/all_to_all | solution.py:366
  46.3 36.8 %copy-start = (bf16[1024,512]{1,0:T(8,128)(2,1)S(1)}, bf16[1024,512]{1,0:T(8,128)(2,1)}, u32[]{:S(2)}) copy-start(bf16[1024,512]{1,0:T(8,128)(2,1)} %constant.19.clone.table_ref) | copy-start | bytes 3145732
  46.3 36.8 %all-to-all-start.1 = ((bf16[128,72,128]{2,1,0:T(8,128)(2,1)}), bf16[128,72,128]{2,1,0:T(8,128)(2,1)S(1)}, u32[]{:S(2)}, u32[]{:S(2)}) async-start(bf16[128,72,128]{2,1,0:T(8,128)(2,1)} %shard_map.75), calls=%async_computation.1 | async-start | bytes 4718592 | tf_op jit(solution)/shard_map/all_to_all | solution.py:369

commit v4 on v3

--- a/solution.py
+++ b/solution.py
@@ -26,8 +26,10 @@
 VALUES = PRODUCTS * PARTS
 ROWS = -(-VALUES // 16) * 16
 APART = ROWS + 8
+SIXTEEN = 16 * PARTS + 8
 WIDE = 8 * ROWS
 
+WHITEN_PIECES = 4
 LEAVE = 32
 
 EPSILON = 1e-06
@@ -36,20 +38,23 @@
 TN = (((0,), (0,)), ((), ()))
 
 
+def bin_order():
+    half = FREQ_BINS // 2
+    return np.concatenate([np.arange(half + 1), np.arange(FREQ_BINS - 1, half, -1)])
+
+
 def dft_table():
-    turns = np.arange(FREQ_BINS)[:, None] * np.arange(SAMPLES)[None, :] % SAMPLES
+    half = FREQ_BINS // 2
+    turns = np.arange(half + 1)[:, None] * np.arange(SAMPLES)[None, :] % SAMPLES
     turns = turns.astype(np.float32) * np.float32(2.0 * math.pi / SAMPLES)
-    table = np.concatenate([np.cos(turns), -np.sin(turns)], axis=0)
+    cosine, sine = np.cos(turns), -np.sin(turns)
+    fill = np.zeros((14, SAMPLES), np.float32)
+    table = np.concatenate([cosine[:half], sine[:half], cosine[half:], sine[half:], fill], axis=0)
     return table.astype(ml_dtypes.bfloat16)
 
 
-def band_table():
-    bin_ids = np.arange(FREQ_BINS)
-    return (np.abs(bin_ids[:, None] - bin_ids[None, :]) <= BAND_HALF).astype(ml_dtypes.bfloat16)
-
-
 def lag_table():
-    bin_ids = np.arange(FREQ_BINS)
+    bin_ids = bin_order()
     lag_ids = np.arange(LAG_BINS) - LAG_BINS // 2
     turns = bin_ids[:, None] * lag_ids[None, :] % SAMPLES
     turns = turns.astype(np.float32) * np.float32(2.0 * math.pi / SAMPLES)
@@ -65,40 +70,51 @@
 
 
 def whiten_kernel(
-    avail_hbm, wave_hbm, dft_hbm, band_hbm, out_ref, avail, wave, dft, band, mixed, avail_sem, wave_sems, dft_sems, band_sem
+    avail_hbm, wave_hbm, dft_hbm, out_hbm, avail, wave, half_dft, dft, mixed, ready, avail_sem, wave_sems, dft_sems, out_sems
 ):
-    runs = lane_runs()
+    half = FREQ_BINS // 2
     wave_copies = [
         pltpu.make_async_copy(wave_hbm.at[pl.ds(row, count)], wave.at[pl.ds(begin, count)], wave_sems.at[i])
-        for i, (row, begin, count) in enumerate(runs)
+        for i, (row, begin, count) in enumerate(lane_runs())
     ]
+    dft_runs = [(p * half, half) for p in range(2)] + [(2 * half, 16)]
     dft_copies = [
-        pltpu.make_async_copy(
-            dft_hbm.at[pl.ds(i * FREQ_BINS, FREQ_BINS)], dft.at[pl.ds(i * FREQ_BINS, FREQ_BINS)], dft_sems.at[i]
-        )
-        for i in range(2)
+        pltpu.make_async_copy(dft_hbm.at[pl.ds(row, count)], half_dft.at[pl.ds(row, count)], dft_sems.at[i])
+        for i, (row, count) in enumerate(dft_runs)
     ]
-    band_copy = pltpu.make_async_copy(band_hbm, band, band_sem)
     avail_copy = pltpu.make_async_copy(avail_hbm, avail, avail_sem)
-    for copy in wave_copies + dft_copies + [band_copy, avail_copy]:
+    for copy in wave_copies + dft_copies + [avail_copy]:
         copy.start()
     wave[LANES:] = jnp.zeros((LANES_FULL - LANES, SAMPLES), jnp.bfloat16)
+
+    def bin_of(row):
+        return jnp.where(row <= half, row, 3 * half - row)
+
+    square = (FREQ_BINS, FREQ_BINS)
+    apart = bin_of(lax.broadcasted_iota(jnp.int32, square, 0)) - bin_of(lax.broadcasted_iota(jnp.int32, square, 1))
+    near = jnp.where(jnp.abs(apart) <= BAND_HALF, 1.0, 0.0).astype(jnp.bfloat16)
     for copy in wave_copies:
         copy.wait()
     waves = wave[...].T
-    dft_copies[0].wait()
+    odd = lax.broadcasted_iota(jnp.int32, (half, SAMPLES), 1) & 1 == 1
+    top = lax.broadcasted_iota(jnp.int32, (half, SAMPLES), 0) == 0
+    for copy in dft_copies:
+        copy.wait()
+    for p in range(2):
+        lower = half_dft[p * half : (p + 1) * half]
+        middle = half_dft[2 * half : 2 * half + 16][p : p + 1]
+        mirrored = jnp.where(odd, -lower, lower) if p == 0 else jnp.where(odd, lower, -lower)
+        dft[p * FREQ_BINS : p * FREQ_BINS + half] = lower
+        dft[p * FREQ_BINS + half : (p + 1) * FREQ_BINS] = jnp.where(top, middle, mirrored)
     real = jnp.dot(dft[:FREQ_BINS], waves, preferred_element_type=jnp.float32)
-    dft_copies[1].wait()
     imag = jnp.dot(dft[FREQ_BINS:], waves, preferred_element_type=jnp.float32)
     power = real * real + imag * imag
     high = power.astype(jnp.bfloat16)
     low = (power - high.astype(jnp.float32)).astype(jnp.bfloat16)
-    band_copy.wait()
-    near = band[...]
     smooth = jnp.dot(near, high, preferred_element_type=jnp.float32) + jnp.dot(
         near, low, preferred_element_type=jnp.float32
     )
-    bin_id = lax.broadcasted_iota(jnp.int32, (FREQ_BINS, 1), 0)
+    bin_id = bin_of(lax.broadcasted_iota(jnp.int32, (FREQ_BINS, 1), 0))
     width = jnp.minimum(bin_id, BAND_HALF) + jnp.minimum(FREQ_BINS - 1 - bin_id, BAND_HALF) + 1
     lane = lax.broadcasted_iota(jnp.int32, (1, LANES_FULL), 1)
     segment = jnp.where(lane < COMPONENTS * 128, lane & 127, 128 + (lane & (SEGMENTS - 129)))
@@ -107,35 +123,43 @@
     mask = ((segment >= first) & (segment < last) & (lane < LANES)).astype(jnp.float32)
     factor = lax.rsqrt(smooth * (1.0 / width.astype(jnp.float32)) + EPSILON) * mask
     spare = jnp.where(lane == LANES, first, jnp.where(lane == LANES + 1, last, 0)).astype(jnp.float32)
-    real = real * factor + spare
-    imag = imag * factor + spare
-    for t in range(LANES_FULL // 128):
-        mixed[t, pl.ds(0, FREQ_BINS, stride=2), :] = real[:, t * 128 : (t + 1) * 128]
-        mixed[t, pl.ds(1, FREQ_BINS, stride=2), :] = imag[:, t * 128 : (t + 1) * 128]
-    for t in range(LANES_FULL // 128):
-        out_ref[:, :, t * 128 : (t + 1) * 128] = mixed[t].astype(jnp.bfloat16).reshape(DEVICES, PARTS, 128)
+    out_copies = []
+    bins = FREQ_BINS // WHITEN_PIECES
+    for i in range(WHITEN_PIECES):
+        rows = slice(i * bins, (i + 1) * bins)
+        for p, values in enumerate((real[rows] * factor[rows] + spare, imag[rows] * factor[rows] + spare)):
+            for t in range(LANES_FULL // 128):
+                mixed[t, pl.ds(2 * i * bins + p, bins, stride=2), :] = values[:, t * 128 : (t + 1) * 128]
+        some = pl.ds(i * bins // BINS, bins // BINS)
+        for t in range(LANES_FULL // 128):
+            values = mixed[t, 2 * i * bins : 2 * (i + 1) * bins, :].astype(jnp.bfloat16)
+            ready[some, :, t * 128 : (t + 1) * 128] = values.reshape(bins // BINS, PARTS, 128)
+        out_copies.append(pltpu.make_async_copy(ready.at[some], out_hbm.at[some], out_sems.at[i]))
+        out_copies[i].start()
+    for copy in out_copies:
+        copy.wait()
 
 
 def whiten(waves, availability):
-    in_hbm = (availability, waves, jnp.asarray(dft_table()), jnp.asarray(band_table()))
     return pl.pallas_call(
         whiten_kernel,
         out_shape=jax.ShapeDtypeStruct((DEVICES, PARTS, LANES_FULL), jnp.bfloat16),
-        in_specs=[pl.BlockSpec(memory_space=pltpu.HBM)] * 4,
-        out_specs=pl.BlockSpec(memory_space=pltpu.VMEM),
+        in_specs=[pl.BlockSpec(memory_space=pltpu.HBM)] * 3,
+        out_specs=pl.BlockSpec(memory_space=pltpu.HBM),
         scratch_shapes=[
             pltpu.SMEM((1, 2), jnp.int32),
             pltpu.VMEM((LANES_FULL, SAMPLES), jnp.bfloat16),
+            pltpu.VMEM((FREQ_BINS + 16, SAMPLES), jnp.bfloat16),
             pltpu.VMEM((2 * FREQ_BINS, SAMPLES), jnp.bfloat16),
-            pltpu.VMEM((FREQ_BINS, FREQ_BINS), jnp.bfloat16),
             pltpu.VMEM((LANES_FULL // 128, 2 * FREQ_BINS, 128), jnp.float32),
+            pltpu.VMEM((DEVICES, PARTS, LANES_FULL), jnp.bfloat16),
             pltpu.SemaphoreType.DMA,
             pltpu.SemaphoreType.DMA((2 * COMPONENTS,)),
-            pltpu.SemaphoreType.DMA((2,)),
-            pltpu.SemaphoreType.DMA,
+            pltpu.SemaphoreType.DMA((3,)),
+            pltpu.SemaphoreType.DMA((WHITEN_PIECES,)),
         ],
-        compiler_params=pltpu.CompilerParams(vmem_limit_bytes=20 * MIB),
-    )(*(pltpu.with_memory_space_constraint(x, pltpu.HBM) for x in in_hbm))
+        compiler_params=pltpu.CompilerParams(vmem_limit_bytes=24 * MIB),
+    )(*(pltpu.with_memory_space_constraint(x, pltpu.HBM) for x in (availability, waves, jnp.asarray(dft_table()))))
 
 
 def route_kernel(slot_ref, order_ref, place_ref, shift_ref):
@@ -190,11 +214,13 @@
     wide = spec_ref[...].astype(jnp.float32).reshape(STATIONS * PARTS, LANES_FULL)
     tiles = LANES_FULL // 128
     for t in range(tiles):
-        spec_full[t] = wide[:, t * 128 : (t + 1) * 128]
+        for high in range(8):
+            rows = wide[high * 16 * PARTS : (high + 1) * 16 * PARTS, t * 128 : (t + 1) * 128]
+            spec_full[t, high * SIXTEEN : high * SIXTEEN + 16 * PARTS] = rows
 
     def part(row, t):
         return jnp.concatenate(
-            [spec_full[t, pl.ds(low * PARTS + row, 8, stride=16 * PARTS), :] for low in range(16)], axis=0
+            [spec_full[t, pl.ds(low * PARTS + row, 8, stride=SIXTEEN), :] for low in range(16)], axis=0
         )
 
     head = part(0, LANES // 128)
@@ -223,7 +249,10 @@
     for f in range(BINS):
         real, imag = fold(2 * f), fold(2 * f + 1)
         real_t, imag_t = real.T, imag.T
-        both = (product(real, real_t) + product(imag, imag_t), product(imag, real_t) - product(real, imag_t))
+        stacked = jnp.concatenate([real, imag], axis=0)
+        by_real, by_imag = product(stacked, real_t), product(stacked, imag_t)
+        size = COMPONENTS * STATIONS
+        both = (by_real[:size] + by_imag[size:], by_real[size:] - by_imag[:size])
         for p in range(2):
             for c in range(COMPONENTS):
                 for d in range(COMPONENTS):
@@ -250,7 +279,7 @@
             target[:, :, k * 128 : (k + 1) * 128] = jnp.concatenate(sides, axis=1).astype(jnp.bfloat16)
         return carry
 
-    lax.fori_loop(0, 8, first_turn, 0, unroll=2)
+    lax.fori_loop(0, 8, first_turn, 0, unroll=8)
 
     pair = lax.broadcasted_iota(jnp.int32, (PER_OWNER, PER_OWNER), 0)
 
@@ -276,7 +305,7 @@
                     targets[high][side, group : group + 8, :] = x[(high - 1) % 8]
         return carry
 
-    lax.fori_loop(0, 8, second_turn, 0)
+    lax.fori_loop(0, 8, second_turn, 0, unroll=8)
 
     def leave(block):
         some = pl.ds(pl.multiple_of(block * LEAVE, LEAVE), LEAVE)
@@ -307,7 +336,7 @@
         in_specs=[pl.BlockSpec(memory_space=pltpu.VMEM)] * 3,
         out_specs=pl.BlockSpec(memory_space=pltpu.HBM),
         scratch_shapes=[
-            pltpu.VMEM((LANES_FULL // 128, STATIONS * PARTS, 128), jnp.float32),
+            pltpu.VMEM((LANES_FULL // 128, 8 * SIXTEEN, 128), jnp.float32),
             pltpu.VMEM((STATIONS * APART, STATIONS), jnp.float32),
             pltpu.VMEM((16, STATIONS, WIDE), jnp.bfloat16),
             pltpu.VMEM((2, WIDE, STATIONS), jnp.bfloat16),
@@ -321,40 +350,45 @@
 
 
 def lag_kernel(owner_ref, cross_ref, table_ref, place_ref, old_hbm, out_hbm, old, new, old_sems, new_sems):
-    old_copies = [pltpu.make_async_copy(old_hbm.at[c], old.at[c], old_sems.at[c]) for c in range(COMPONENTS)]
-    new_copies = [pltpu.make_async_copy(new.at[c], out_hbm.at[c], new_sems.at[c]) for c in range(COMPONENTS)]
-    for copy in old_copies:
+    old_copies = [[pltpu.make_async_copy(old_hbm.at[c, d], old.at[c, d], old_sems.at[c, d]) for d in range(COMPONENTS)] for c in range(COMPONENTS)]
+    for copy in sum(old_copies, []):
         copy.start()
     row = lax.broadcasted_iota(jnp.int32, (PER_OWNER, PER_OWNER), 0)
     chosen = jnp.where(row == place_ref[pl.ds(owner_ref[0], 1), :], 1.0, 0.0).astype(jnp.bfloat16)
+    new_copies = []
     for c in range(COMPONENTS):
         rows = []
-        for cd in range(c * COMPONENTS, (c + 1) * COMPONENTS):
-            spectra = cross_ref[:, cd * PARTS : (cd + 1) * PARTS, :].reshape(2 * FREQ_BINS, PER_OWNER)
+        for d in range(COMPONENTS):
+            begin = (c * COMPONENTS + d) * PARTS
+            spectra = cross_ref[:, begin : begin + PARTS, :].reshape(2 * FREQ_BINS, PER_OWNER)
             turned = lax.dot_general(chosen, spectra, NT, preferred_element_type=jnp.float32)
             rows.append(turned.astype(jnp.bfloat16))
         lagged = jnp.dot(jnp.concatenate(rows, axis=0), table_ref[...], preferred_element_type=jnp.float32)
-        old_copies[c].wait()
-        new[c] = old[c] + lagged.reshape(COMPONENTS, PER_OWNER, LAG_BINS)
-        new_copies[c].start()
+        new[c] = lagged.reshape(COMPONENTS, PER_OWNER, LAG_BINS)
+        for e in ((), (0, 1), (2,))[c]:
+            for d in range(COMPONENTS):
+                old_copies[e][d].wait()
+                new[e, d] = old[e, d] + new[e, d]
+                copy = pltpu.make_async_copy(new.at[e, d], out_hbm.at[e, d], new_sems.at[e, d])
+                copy.start()
+                new_copies.append(copy)
     for copy in new_copies:
         copy.wait()
 
 
 def lag(owner, arrived, place, old_rows):
-    shape = (COMPONENTS, COMPONENTS, PER_OWNER, LAG_BINS)
     return pl.pallas_call(
         lag_kernel,
-        out_shape=jax.ShapeDtypeStruct(shape, jnp.float32),
+        out_shape=jax.ShapeDtypeStruct(old_rows.shape, jnp.float32),
         in_specs=[pl.BlockSpec(memory_space=pltpu.SMEM)]
         + [pl.BlockSpec(memory_space=pltpu.VMEM)] * 3
         + [pl.BlockSpec(memory_space=pltpu.HBM)],
         out_specs=pl.BlockSpec(memory_space=pltpu.HBM),
         scratch_shapes=[
-            pltpu.VMEM(shape, jnp.float32),
-            pltpu.VMEM(shape, jnp.float32),
-            pltpu.SemaphoreType.DMA((COMPONENTS,)),
-            pltpu.SemaphoreType.DMA((COMPONENTS,)),
+            pltpu.VMEM(old_rows.shape, jnp.float32),
+            pltpu.VMEM(old_rows.shape, jnp.float32),
+            pltpu.SemaphoreType.DMA((COMPONENTS, COMPONENTS)),
+            pltpu.SemaphoreType.DMA((COMPONENTS, COMPONENTS)),
         ],
         compiler_params=pltpu.CompilerParams(vmem_limit_bytes=24 * MIB),
     )(owner, arrived, jnp.asarray(lag_table()), place, pltpu.with_memory_space_constraint(old_rows, pltpu.HBM))

time: 87.3 us -> 84.7 us (0.970)
  Pallas kernels: 26.2 us -> 23.6 us
    pallas_call x1, Pallas kernels: 9.99 us -> 8.6 us  [cross(): pl.pallas_call(cross_kernel, out_shape=jax.ShapeDtypeStruct((DEVICES, VAL...]
where the time goes in v4:
time: 84.7 us; the launch traced here: 84.5 us
  waiting for transfers between devices  44.1 us (52%)
  Pallas kernels  23.6 us (28%)
  starting transfers between devices  15.9 us (19%)
    all_to_all x1, waiting for transfers between devices, local(): lax.all_to_all(crossed, axes, split_axis=0, concat_axis=0, tiled=True)  32.4 us
    all_to_all x1, waiting for transfers between devices, local(): lax.all_to_all(spectra, axes, split_axis=0, concat_axis=0, tiled=True)  11.7 us
    all_to_all x1, starting transfers between devices, local(): lax.all_to_all(spectra, axes, split_axis=0, concat_axis=0, tiled=True)  11.5 us
    pallas_call x1, Pallas kernels, cross(): pl.pallas_call(cross_kernel, out_shape=jax.ShapeDtypeStruct((DEVICES, VAL...  8.6 us
    pallas_call x1, Pallas kernels, route(): pl.pallas_call(route_kernel, out_shape=(table, table, jax.ShapeDtypeStruc...  6.77 us
    pallas_call x1, Pallas kernels, whiten(): pl.pallas_call(whiten_kernel, out_shape=jax.ShapeDtypeStruct((DEVICES, PA...  4.9 us
    all_to_all x1, starting transfers between devices, local(): lax.all_to_all(crossed, axes, split_axis=0, concat_axis=0, tiled=True)  4.42 us
    pallas_call x1, Pallas kernels, lag(): pl.pallas_call(lag_kernel, out_shape=jax.ShapeDtypeStruct(old_rows.shape,...  3.37 us
  transfers between devices with their start and end apart: 2, of which 2 were waited for; matrix products, arithmetic and copies ran while one was open for 1% of the time, Pallas kernels for 8%

profile of v4, /device:TPU:1, one launch (start us, length us, event | category | flops | bytes accessed | tf_op | source)
XLA Modules:
  0.0 84.5 jit_solution(17953689930725501834)
XLA Ops:
  0.0 0.0 copy-start.1
  0.0 4.9 %shard_map.65 = bf16[128,8,512]{2,1,0:T(8,128)(2,1)} custom-call(s32[1,2]{1,0:T(1,128)} %avail_hbm.1, bf16[480,1024]{1,0:T(8,128)(2,1)} %bitcast.13, bf16[528,1024]{1,0:T(8,128)(2,1)} %constant.15.clone.dft_hbm), custom_call_target="tpu_custom_call" | custom-call | tf_op jit(solution)/shard_map/pallas_call | solution.py:144
  4.9 11.5 %all-to-all-start = ((bf16[128,8,512]{2,1,0:T(8,128)(2,1)}), bf16[128,8,512]{2,1,0:T(8,128)(2,1)S(1)}, u32[]{:S(2)}, u32[]{:S(2)}) async-start(bf16[128,8,512]{2,1,0:T(8,128)(2,1)} %shard_map.65), calls=%async_computation | async-start | bytes 2097152 | tf_op jit(solution)/shard_map/all_to_all | solution.py:400
  16.4 0.0 copy-done.1
  16.4 0.2 reshape.13
  16.6 0.3 copy.11
  16.9 0.2 reshape.14
  17.1 0.1 copy.9.slot_ref
  17.2 6.8 %shard_map.64 = (s32[128,128]{1,0:T(8,128)S(1)}, s32[128,128]{1,0:T(8,128)S(1)}, s32[8,128]{1,0:T(8,128)S(1)}) custom-call(s32[128,128]{1,0:T(8,128)S(1)} %copy.9.slot_ref), custom_call_target="tpu_custom_call" | custom-call | flops 40000000 | bytes 200000 | tf_op jit(solution)/shard_map/pallas_call | solution.py:201
  24.0 11.7 %all-to-all-done.spec_ref = bf16[128,8,512]{2,1,0:T(8,128)(2,1)S(1)} async-done(((bf16[128,8,512]{2,1,0:T(8,128)(2,1)}), bf16[128,8,512]{2,1,0:T(8,128)(2,1)S(1)}, u32[]{:S(2)}, u32[]{:S(2)}) %all-to-all-start) | async-done | bytes 1048608 | tf_op jit(solution)/shard_map/all_to_all | solution.py:400
  35.7 8.6 %shard_map.66 = bf16[128,72,128]{2,1,0:T(8,128)(2,1)} custom-call(s32[128,128]{1,0:T(8,128)S(1)} %get-tuple-element.8.order_ref, s32[8,128]{1,0:T(8,128)S(1)} %get-tuple-element.9.shift_ref, bf16[128,8,512]{2,1,0:T(8,128)(2,1)S(1)} %all-to-all-done.spec_ref), custom_call_target="tpu_custom_call" | custom-call | tf_op jit(solution)/shard_map/pallas_call | solution.py:333
  44.3 0.0 copy-start
  44.3 4.4 %all-to-all-start.1 = ((bf16[128,72,128]{2,1,0:T(8,128)(2,1)}), bf16[128,72,128]{2,1,0:T(8,128)(2,1)S(1)}, u32[]{:S(2)}, u32[]{:S(2)}) async-start(bf16[128,72,128]{2,1,0:T(8,128)(2,1)} %shard_map.66), calls=%async_computation.1 | async-start | bytes 4718592 | tf_op jit(solution)/shard_map/all_to_all | solution.py:403
  48.8 32.4 %all-to-all-done.1.cross_ref = bf16[128,72,128]{2,1,0:T(8,128)(2,1)S(1)} async-done(((bf16[128,72,128]{2,1,0:T(8,128)(2,1)}), bf16[128,72,128]{2,1,0:T(8,128)(2,1)S(1)}, u32[]{:S(2)}, u32[]{:S(2)}) %all-to-all-start.1) | async-done | bytes 2359328 | tf_op jit(solution)/shard_map/all_to_all | solution.py:403
  81.1 0.0 copy-done
  81.1 3.4 %shard_map.67 = f32[3,3,128,512]{3,2,1,0:T(8,128)} custom-call(s32[1]{0:T(128)} %bitcast.owner_ref, bf16[128,72,128]{2,1,0:T(8,128)(2,1)S(1)} %all-to-all-done.1.cross_ref, bf16[1024,512]{1,0:T(8,128)(2,1)S(1)} %copy-done, s32[128,128]{1,0:T(8,128)S(1)} %get-tuple-element.10.place_ref, f32[3,3,128,512]{3,2,1,0:T(8,128)} %bitcast.11), custom_call_target="tpu_custom_call" | custom-call | tf_op jit(solution)/shard_map/pallas_call | solution.py:380
Async XLA Ops:
  0.0 16.4 %copy-start.1 = (s32[128,128]{1,0:T(8,128)S(1)}, s32[128,128]{1,0:T(8,128)}, u32[]{:S(2)}) copy-start(s32[128,128]{1,0:T(8,128)} %param.8) | copy-start | bytes 196612
  4.9 30.8 %all-to-all-start = ((bf16[128,8,512]{2,1,0:T(8,128)(2,1)}), bf16[128,8,512]{2,1,0:T(8,128)(2,1)S(1)}, u32[]{:S(2)}, u32[]{:S(2)}) async-start(bf16[128,8,512]{2,1,0:T(8,128)(2,1)} %shard_map.65), calls=%async_computation | async-start | bytes 2097152 | tf_op jit(solution)/shard_map/all_to_all | solution.py:400
  44.3 36.8 %copy-start = (bf16[1024,512]{1,0:T(8,128)(2,1)S(1)}, bf16[1024,512]{1,0:T(8,128)(2,1)}, u32[]{:S(2)}) copy-start(bf16[1024,512]{1,0:T(8,128)(2,1)} %constant.16.clone.table_ref) | copy-start | bytes 3145732
  44.3 36.8 %all-to-all-start.1 = ((bf16[128,72,128]{2,1,0:T(8,128)(2,1)}), bf16[128,72,128]{2,1,0:T(8,128)(2,1)S(1)}, u32[]{:S(2)}, u32[]{:S(2)}) async-start(bf16[128,72,128]{2,1,0:T(8,128)(2,1)} %shard_map.66), calls=%async_computation.1 | async-start | bytes 4718592 | tf_op jit(solution)/shard_map/all_to_all | solution.py:403

commit v5 on v4

--- a/solution.py
+++ b/solution.py
@@ -143,7 +143,7 @@
 def whiten(waves, availability):
     return pl.pallas_call(
         whiten_kernel,
-        out_shape=jax.ShapeDtypeStruct((DEVICES, PARTS, LANES_FULL), jnp.bfloat16),
+        out_shape=pltpu.HBM((DEVICES, PARTS, LANES_FULL), jnp.bfloat16),
         in_specs=[pl.BlockSpec(memory_space=pltpu.HBM)] * 3,
         out_specs=pl.BlockSpec(memory_space=pltpu.HBM),
         scratch_shapes=[
@@ -162,7 +162,7 @@
     )(*(pltpu.with_memory_space_constraint(x, pltpu.HBM) for x in (availability, waves, jnp.asarray(dft_table()))))
 
 
-def route_kernel(slot_ref, order_ref, place_ref, shift_ref):
+def route_kernel(slot_ref, chosen_hbm, place_ref, shift_ref, order, chosen, chosen_sems):
     shape = (DEVICES, PER_OWNER)
     tile = lax.broadcasted_iota(jnp.int32, shape, 0)
     lane = lax.broadcasted_iota(jnp.int32, shape, 1)
@@ -186,13 +186,29 @@
         return found
 
     ordered = lax.fori_loop(0, PER_OWNER // 8, pick, jnp.zeros(shape, jnp.int32))
-    order_ref[...] = (ordered >> 7) & (PER_OWNER - 1)
+    order[...] = (ordered >> 7) & (PER_OWNER - 1)
+    row = lax.broadcasted_iota(jnp.int32, shape, 0)
+
+    def leave(block):
+        some = pl.ds(block * 16, 16)
+        return pltpu.make_async_copy(chosen.at[some], chosen_hbm.at[some], chosen_sems.at[block])
+
+    def choose(block, carry):
+        target, source = chosen.at[pl.ds(block * 16, 16)], order.at[pl.ds(pl.multiple_of(block * 16, 16), 16)]
+        for i in range(16):
+            target[i] = jnp.where(row == source[i : i + 1, :], 1.0, 0.0).astype(jnp.bfloat16)
+        leave(block).start()
+        return carry
+
+    lax.fori_loop(0, 8, choose, 0)
     shift = (ordered >> 14) & (DEVICES - 1)
     shift_ref[...] = shift[:8]
     slot = ordered & (PER_OWNER - 1)
     for bit in range(7):
         slot = jnp.where((shift >> bit) & 1 == 1, pltpu.roll(slot, 1 << bit, 0), slot)
     place_ref[...] = slot
+    for block in range(8):
+        leave(block).wait()
 
 
 def route(pair_slot):
@@ -200,17 +216,45 @@
     table = jax.ShapeDtypeStruct((DEVICES, PER_OWNER), jnp.int32)
     return pl.pallas_call(
         route_kernel,
-        out_shape=(table, table, jax.ShapeDtypeStruct((8, PER_OWNER), jnp.int32)),
+        out_shape=(
+            pltpu.HBM((DEVICES, PER_OWNER, PER_OWNER), jnp.bfloat16),
+            table,
+            jax.ShapeDtypeStruct((8, PER_OWNER), jnp.int32),
+        ),
         in_specs=[pl.BlockSpec(memory_space=pltpu.VMEM)],
-        out_specs=[pl.BlockSpec(memory_space=pltpu.VMEM)] * 3,
-        compiler_params=pltpu.CompilerParams(vmem_limit_bytes=4 * MIB),
+        out_specs=[pl.BlockSpec(memory_space=pltpu.HBM)] + [pl.BlockSpec(memory_space=pltpu.VMEM)] * 2,
+        scratch_shapes=[
+            pltpu.VMEM((DEVICES, PER_OWNER), jnp.int32),
+            pltpu.VMEM((DEVICES, PER_OWNER, PER_OWNER), jnp.bfloat16),
+            pltpu.SemaphoreType.DMA((8,)),
+        ],
+        compiler_params=pltpu.CompilerParams(vmem_limit_bytes=10 * MIB),
         cost_estimate=pl.CostEstimate(flops=40_000_000, bytes_accessed=200_000, transcendentals=0),
     )(tiles)
 
 
 def cross_kernel(
-    order_ref, shift_ref, spec_ref, out_hbm, spec_full, planes, columns, turned, placed, moved, ready, out_sems
+    chosen_hbm,
+    shift_ref,
+    spec_ref,
+    out_hbm,
+    spec_full,
+    planes,
+    columns,
+    turned,
+    placed,
+    moved,
+    ready,
+    chosen,
+    chosen_sems,
+    out_sems,
 ):
+    chosen_copies = [
+        pltpu.make_async_copy(chosen_hbm.at[pl.ds(i * 32, 32)], chosen.at[pl.ds(i * 32, 32)], chosen_sems.at[i])
+        for i in range(4)
+    ]
+    for copy in chosen_copies:
+        copy.start()
     wide = spec_ref[...].astype(jnp.float32).reshape(STATIONS * PARTS, LANES_FULL)
     tiles = LANES_FULL // 128
     for t in range(tiles):
@@ -281,7 +325,8 @@
 
     lax.fori_loop(0, 8, first_turn, 0, unroll=8)
 
-    pair = lax.broadcasted_iota(jnp.int32, (PER_OWNER, PER_OWNER), 0)
+    for copy in chosen_copies:
+        copy.wait()
 
     def second_turn(i, carry):
         source = columns.at[pl.ds(2 * i, 2)]
@@ -291,11 +336,9 @@
         targets = [moved.at[pl.ds(high * 16 + 2 * i, 2)] for high in range(9)]
         for side in range(2):
             for high in range(8):
-                order = order_ref[pl.ds(high * 16 + 2 * i + side, 1), :]
-                chosen = jnp.where(pair == order, 1.0, 0.0).astype(jnp.bfloat16)
                 values = turned[side, high * ROWS : (high + 1) * ROWS, :]
                 placed[side, high * ROWS : (high + 1) * ROWS, :] = jnp.dot(
-                    values, chosen, preferred_element_type=jnp.float32
+                    values, chosen[high * 16 + 2 * i + side], preferred_element_type=jnp.float32
                 )
             for group in range(0, VALUES, 8):
                 x = [placed[side, high * ROWS + group : high * ROWS + group + 8, :] for high in range(8)]
@@ -329,11 +372,11 @@
         leave(block).wait()
 
 
-def cross(order, shift, spectra):
+def cross(chosen, shift, spectra):
     return pl.pallas_call(
         cross_kernel,
-        out_shape=jax.ShapeDtypeStruct((DEVICES, VALUES, PER_OWNER), jnp.bfloat16),
-        in_specs=[pl.BlockSpec(memory_space=pltpu.VMEM)] * 3,
+        out_shape=pltpu.HBM((DEVICES, VALUES, PER_OWNER), jnp.bfloat16),
+        in_specs=[pl.BlockSpec(memory_space=pltpu.HBM)] + [pl.BlockSpec(memory_space=pltpu.VMEM)] * 2,
         out_specs=pl.BlockSpec(memory_space=pltpu.HBM),
         scratch_shapes=[
             pltpu.VMEM((LANES_FULL // 128, 8 * SIXTEEN, 128), jnp.float32),
@@ -343,10 +386,12 @@
             pltpu.VMEM((2, WIDE, STATIONS), jnp.float32),
             pltpu.VMEM((DEVICES + 16, VALUES, PER_OWNER), jnp.float32),
             pltpu.VMEM((DEVICES, VALUES, PER_OWNER), jnp.bfloat16),
+            pltpu.VMEM((DEVICES, PER_OWNER, PER_OWNER), jnp.bfloat16),
+            pltpu.SemaphoreType.DMA((4,)),
             pltpu.SemaphoreType.DMA((DEVICES // LEAVE,)),
         ],
-        compiler_params=pltpu.CompilerParams(vmem_limit_bytes=28 * MIB),
-    )(order, shift, spectra)
+        compiler_params=pltpu.CompilerParams(vmem_limit_bytes=32 * MIB),
+    )(pltpu.with_memory_space_constraint(chosen, pltpu.HBM), shift, spectra)
 
 
 def lag_kernel(owner_ref, cross_ref, table_ref, place_ref, old_hbm, out_hbm, old, new, old_sems, new_sems):
@@ -379,7 +424,7 @@
 def lag(owner, arrived, place, old_rows):
     return pl.pallas_call(
         lag_kernel,
-        out_shape=jax.ShapeDtypeStruct(old_rows.shape, jnp.float32),
+        out_shape=pltpu.HBM(old_rows.shape, jnp.float32),
         in_specs=[pl.BlockSpec(memory_space=pltpu.SMEM)]
         + [pl.BlockSpec(memory_space=pltpu.VMEM)] * 3
         + [pl.BlockSpec(memory_space=pltpu.HBM)],
@@ -398,8 +443,8 @@
     axes = ("row", "col")
     spectra = whiten(waveforms.reshape(LANES, SAMPLES), availability)
     spectra = lax.all_to_all(spectra, axes, split_axis=0, concat_axis=0, tiled=True)
-    order, place, shift = route(pair_slot)
-    crossed = cross(order, shift, spectra)
+    chosen, place, shift = route(pair_slot)
+    crossed = cross(chosen, shift, spectra)
     arrived = lax.all_to_all(crossed, axes, split_axis=0, concat_axis=0, tiled=True)
     old_rows = jnp.transpose(old_stack, (1, 2, 0, 3))
     owner = (lax.axis_index("row") * lax.axis_size("col") + lax.axis_index("col")).astype(jnp.int32).reshape(1)

time: 84.7 us -> 83.5 us (0.986)
  waiting for transfers between devices: 44.1 us -> 42 us
    all_to_all x1, waiting for transfers between devices: 11.7 us -> 9.65 us  [local(): lax.all_to_all(spectra, axes, split_axis=0, concat_axis=0, tiled=True)]
  transfers between devices with their start and end apart: 2 -> 2, of which waited for: 2 -> 2; matrix products, arithmetic and copies ran while one was open for 1% -> 1% of each run, Pallas kernels for 8% -> 11%
where the time goes in v5:
time: 83.5 us; the launch traced here: 83.3 us
  waiting for transfers between devices  42 us (50%)
  Pallas kernels  24.4 us (29%)
  starting transfers between devices  15.9 us (19%)
    all_to_all x1, waiting for transfers between devices, local(): lax.all_to_all(crossed, axes, split_axis=0, concat_axis=0, tiled=True)  32.4 us
    all_to_all x1, starting transfers between devices, local(): lax.all_to_all(spectra, axes, split_axis=0, concat_axis=0, tiled=True)  11.5 us
    all_to_all x1, waiting for transfers between devices, local(): lax.all_to_all(spectra, axes, split_axis=0, concat_axis=0, tiled=True)  9.65 us
    pallas_call x1, Pallas kernels, route(): pl.pallas_call(route_kernel, out_shape=(pltpu.HBM((DEVICES, PER_OWNER, PE...  8.83 us
    pallas_call x1, Pallas kernels, cross(): pl.pallas_call(cross_kernel, out_shape=pltpu.HBM((DEVICES, VALUES, PER_OW...  7.34 us
    pallas_call x1, Pallas kernels, whiten(): pl.pallas_call(whiten_kernel, out_shape=pltpu.HBM((DEVICES, PARTS, LANES_...  4.9 us
    all_to_all x1, starting transfers between devices, local(): lax.all_to_all(crossed, axes, split_axis=0, concat_axis=0, tiled=True)  4.42 us
    pallas_call x1, Pallas kernels, lag(): pl.pallas_call(lag_kernel, out_shape=pltpu.HBM(old_rows.shape, jnp.float3...  3.38 us
  transfers between devices with their start and end apart: 2, of which 2 were waited for; matrix products, arithmetic and copies ran while one was open for 1% of the time, Pallas kernels for 11%

profile of v5, /device:TPU:1, one launch (start us, length us, event | category | flops | bytes accessed | tf_op | source)
XLA Modules:
  0.0 83.3 jit_solution(3885248002644139713)
XLA Ops:
  0.0 0.0 copy-start.1
  0.0 4.9 %shard_map.65 = bf16[128,8,512]{2,1,0:T(8,128)(2,1)} custom-call(s32[1,2]{1,0:T(1,128)} %avail_hbm.1, bf16[480,1024]{1,0:T(8,128)(2,1)} %bitcast.13, bf16[528,1024]{1,0:T(8,128)(2,1)} %constant.15.clone.dft_hbm), custom_call_target="tpu_custom_call" | custom-call | tf_op jit(solution)/shard_map/pallas_call | solution.py:144
  4.9 11.5 %all-to-all-start = ((bf16[128,8,512]{2,1,0:T(8,128)(2,1)}), bf16[128,8,512]{2,1,0:T(8,128)(2,1)S(1)}, u32[]{:S(2)}, u32[]{:S(2)}) async-start(bf16[128,8,512]{2,1,0:T(8,128)(2,1)} %shard_map.65), calls=%async_computation | async-start | bytes 2097152 | tf_op jit(solution)/shard_map/all_to_all | solution.py:445
  16.4 0.0 copy-done.1
  16.4 0.2 reshape.13
  16.6 0.3 copy.11
  16.9 0.2 reshape.14
  17.1 0.1 copy.9.slot_ref
  17.2 8.8 %shard_map.64 = (bf16[128,128,128]{2,1,0:T(8,128)(2,1)}, s32[128,128]{1,0:T(8,128)S(1)}, s32[8,128]{1,0:T(8,128)S(1)}) custom-call(s32[128,128]{1,0:T(8,128)S(1)} %copy.9.slot_ref), custom_call_target="tpu_custom_call" | custom-call | flops 40000000 | bytes 200000 | tf_op jit(solution)/shard_map/pallas_call | solution.py:217
  26.1 9.7 %all-to-all-done.spec_ref = bf16[128,8,512]{2,1,0:T(8,128)(2,1)S(1)} async-done(((bf16[128,8,512]{2,1,0:T(8,128)(2,1)}), bf16[128,8,512]{2,1,0:T(8,128)(2,1)S(1)}, u32[]{:S(2)}, u32[]{:S(2)}) %all-to-all-start) | async-done | bytes 1048608 | tf_op jit(solution)/shard_map/all_to_all | solution.py:445
  35.7 7.3 %shard_map.66 = bf16[128,72,128]{2,1,0:T(8,128)(2,1)} custom-call(bf16[128,128,128]{2,1,0:T(8,128)(2,1)} %get-tuple-element.8.chosen_hbm, s32[8,128]{1,0:T(8,128)S(1)} %get-tuple-element.9.shift_ref, bf16[128,8,512]{2,1,0:T(8,128)(2,1)S(1)} %all-to-all-done.spec_ref), custom_call_target="tpu_custom_call" | custom-call | tf_op jit(solution)/shard_map/pallas_call | solution.py:376
  43.1 0.0 copy-start
  43.1 4.4 %all-to-all-start.1 = ((bf16[128,72,128]{2,1,0:T(8,128)(2,1)}), bf16[128,72,128]{2,1,0:T(8,128)(2,1)S(1)}, u32[]{:S(2)}, u32[]{:S(2)}) async-start(bf16[128,72,128]{2,1,0:T(8,128)(2,1)} %shard_map.66), calls=%async_computation.1 | async-start | bytes 4718592 | tf_op jit(solution)/shard_map/all_to_all | solution.py:448
  47.5 32.4 %all-to-all-done.1.cross_ref = bf16[128,72,128]{2,1,0:T(8,128)(2,1)S(1)} async-done(((bf16[128,72,128]{2,1,0:T(8,128)(2,1)}), bf16[128,72,128]{2,1,0:T(8,128)(2,1)S(1)}, u32[]{:S(2)}, u32[]{:S(2)}) %all-to-all-start.1) | async-done | bytes 2359328 | tf_op jit(solution)/shard_map/all_to_all | solution.py:448
  79.9 0.0 copy-done
  79.9 3.4 %shard_map.67 = f32[3,3,128,512]{3,2,1,0:T(8,128)} custom-call(s32[1]{0:T(128)} %bitcast.owner_ref, bf16[128,72,128]{2,1,0:T(8,128)(2,1)S(1)} %all-to-all-done.1.cross_ref, bf16[1024,512]{1,0:T(8,128)(2,1)S(1)} %copy-done, s32[128,128]{1,0:T(8,128)S(1)} %get-tuple-element.10.place_ref, f32[3,3,128,512]{3,2,1,0:T(8,128)} %bitcast.11), custom_call_target="tpu_custom_call" | custom-call | tf_op jit(solution)/shard_map/pallas_call | solution.py:425
Async XLA Ops:
  0.0 16.4 %copy-start.1 = (s32[128,128]{1,0:T(8,128)S(1)}, s32[128,128]{1,0:T(8,128)}, u32[]{:S(2)}) copy-start(s32[128,128]{1,0:T(8,128)} %param.8) | copy-start | bytes 196612
  4.9 30.8 %all-to-all-start = ((bf16[128,8,512]{2,1,0:T(8,128)(2,1)}), bf16[128,8,512]{2,1,0:T(8,128)(2,1)S(1)}, u32[]{:S(2)}, u32[]{:S(2)}) async-start(bf16[128,8,512]{2,1,0:T(8,128)(2,1)} %shard_map.65), calls=%async_computation | async-start | bytes 2097152 | tf_op jit(solution)/shard_map/all_to_all | solution.py:445
  43.1 36.8 %copy-start = (bf16[1024,512]{1,0:T(8,128)(2,1)S(1)}, bf16[1024,512]{1,0:T(8,128)(2,1)}, u32[]{:S(2)}) copy-start(bf16[1024,512]{1,0:T(8,128)(2,1)} %constant.16.clone.table_ref) | copy-start | bytes 3145732
  43.1 36.8 %all-to-all-start.1 = ((bf16[128,72,128]{2,1,0:T(8,128)(2,1)}), bf16[128,72,128]{2,1,0:T(8,128)(2,1)S(1)}, u32[]{:S(2)}, u32[]{:S(2)}) async-start(bf16[128,72,128]{2,1,0:T(8,128)(2,1)} %shard_map.66), calls=%async_computation.1 | async-start | bytes 4718592 | tf_op jit(solution)/shard_map/all_to_all | solution.py:448

commit v6 on v5

--- a/solution.py
+++ b/solution.py
@@ -290,26 +290,35 @@
     def product(x, y):
         return jnp.dot(x, y, preferred_element_type=jnp.float32)
 
-    for f in range(BINS):
-        real, imag = fold(2 * f), fold(2 * f + 1)
-        real_t, imag_t = real.T, imag.T
-        stacked = jnp.concatenate([real, imag], axis=0)
-        by_real, by_imag = product(stacked, real_t), product(stacked, imag_t)
-        size = COMPONENTS * STATIONS
-        both = (by_real[:size] + by_imag[size:], by_real[size:] - by_imag[:size])
-        for p in range(2):
-            for c in range(COMPONENTS):
-                for d in range(COMPONENTS):
-                    plane = both[p][c * STATIONS : (c + 1) * STATIONS, d * STATIONS : (d + 1) * STATIONS]
-                    row = (c * COMPONENTS + d) * PARTS + 2 * f + p
-                    planes[pl.ds(row, STATIONS, stride=APART), :] = plane * scale
+    folded = [(fold(2 * f), fold(2 * f + 1)) for f in range(BINS)]
+    folded_t = [(real.T, imag.T) for real, imag in folded]
+
+    def multiply(begin, count):
+        for f in range(BINS):
+            stacked = jnp.concatenate(
+                [
+                    side[c * STATIONS + begin : c * STATIONS + begin + count]
+                    for side in folded[f]
+                    for c in range(COMPONENTS)
+                ],
+                axis=0,
+            )
+            by_real, by_imag = product(stacked, folded_t[f][0]), product(stacked, folded_t[f][1])
+            size = COMPONENTS * count
+            both = (by_real[:size] + by_imag[size:], by_real[size:] - by_imag[:size])
+            for p in range(2):
+                for c in range(COMPONENTS):
+                    for d in range(COMPONENTS):
+                        plane = both[p][c * count : (c + 1) * count, d * STATIONS : (d + 1) * STATIONS]
+                        row = (c * COMPONENTS + d) * PARTS + 2 * f + p
+                        planes[pl.ds(begin * APART + row, count, stride=APART), :] = plane * scale[begin : begin + count]
 
     moves = [(shift_ref[...] >> bit) & 1 == 1 for bit in range(7)]
 
-    def first_turn(i, carry):
+    def first_turn(i):
         two = 16 * APART
-        source = planes.at[pl.ds(pl.multiple_of(i * two, 8), two)]
-        target = columns.at[:, pl.ds(pl.multiple_of(i * 16, 16), 16)]
+        source = planes.at[pl.ds(i * two, two)]
+        target = columns.at[:, pl.ds(i * 16, 16)]
         for k in range(WIDE // 128):
             sides = []
             for side in range(2):
@@ -321,9 +330,11 @@
                 rows = jnp.concatenate(rows, axis=0).astype(jnp.bfloat16).T
                 sides.append(rows.astype(jnp.float32).reshape(16, 8, 128))
             target[:, :, k * 128 : (k + 1) * 128] = jnp.concatenate(sides, axis=1).astype(jnp.bfloat16)
-        return carry
-
-    lax.fori_loop(0, 8, first_turn, 0, unroll=8)
+
+    for block in range(2):
+        multiply(block * STATIONS // 2, STATIONS // 2)
+        for i in range(4 * block, 4 * block + 4):
+            first_turn(i)
 
     for copy in chosen_copies:
         copy.wait()

time: 83.5 us -> 82.7 us (level)
  no operation moved by 1% of the time
where the time goes in v6:
time: 82.7 us; the launch traced here: 82.5 us
  waiting for transfers between devices  42 us (51%)
  Pallas kernels  23.7 us (29%)
  starting transfers between devices  15.9 us (19%)
    all_to_all x1, waiting for transfers between devices, local(): lax.all_to_all(crossed, axes, split_axis=0, concat_axis=0, tiled=True)  32.4 us
    all_to_all x1, starting transfers between devices, local(): lax.all_to_all(spectra, axes, split_axis=0, concat_axis=0, tiled=True)  11.5 us
    all_to_all x1, waiting for transfers between devices, local(): lax.all_to_all(spectra, axes, split_axis=0, concat_axis=0, tiled=True)  9.65 us
    pallas_call x1, Pallas kernels, route(): pl.pallas_call(route_kernel, out_shape=(pltpu.HBM((DEVICES, PER_OWNER, PE...  8.83 us
    pallas_call x1, Pallas kernels, cross(): pl.pallas_call(cross_kernel, out_shape=pltpu.HBM((DEVICES, VALUES, PER_OW...  6.57 us
    pallas_call x1, Pallas kernels, whiten(): pl.pallas_call(whiten_kernel, out_shape=pltpu.HBM((DEVICES, PARTS, LANES_...  4.9 us
    all_to_all x1, starting transfers between devices, local(): lax.all_to_all(crossed, axes, split_axis=0, concat_axis=0, tiled=True)  4.42 us
    pallas_call x1, Pallas kernels, lag(): pl.pallas_call(lag_kernel, out_shape=pltpu.HBM(old_rows.shape, jnp.float3...  3.38 us
  transfers between devices with their start and end apart: 2, of which 2 were waited for; matrix products, arithmetic and copies ran while one was open for 1% of the time, Pallas kernels for 11%

profile of v6, /device:TPU:1, one launch (start us, length us, event | category | flops | bytes accessed | tf_op | source)
XLA Modules:
  0.0 82.5 jit_solution(9103410998696476038)
XLA Ops:
  0.0 0.0 copy-start.1
  0.0 4.9 %shard_map.65 = bf16[128,8,512]{2,1,0:T(8,128)(2,1)} custom-call(s32[1,2]{1,0:T(1,128)} %avail_hbm.1, bf16[480,1024]{1,0:T(8,128)(2,1)} %bitcast.13, bf16[528,1024]{1,0:T(8,128)(2,1)} %constant.15.clone.dft_hbm), custom_call_target="tpu_custom_call" | custom-call | tf_op jit(solution)/shard_map/pallas_call | solution.py:144
  4.9 11.5 %all-to-all-start = ((bf16[128,8,512]{2,1,0:T(8,128)(2,1)}), bf16[128,8,512]{2,1,0:T(8,128)(2,1)S(1)}, u32[]{:S(2)}, u32[]{:S(2)}) async-start(bf16[128,8,512]{2,1,0:T(8,128)(2,1)} %shard_map.65), calls=%async_computation | async-start | bytes 2097152 | tf_op jit(solution)/shard_map/all_to_all | solution.py:456
  16.4 0.0 copy-done.1
  16.4 0.2 reshape.13
  16.6 0.3 copy.11
  16.9 0.2 reshape.14
  17.1 0.1 copy.9.slot_ref
  17.2 8.8 %shard_map.64 = (bf16[128,128,128]{2,1,0:T(8,128)(2,1)}, s32[128,128]{1,0:T(8,128)S(1)}, s32[8,128]{1,0:T(8,128)S(1)}) custom-call(s32[128,128]{1,0:T(8,128)S(1)} %copy.9.slot_ref), custom_call_target="tpu_custom_call" | custom-call | flops 40000000 | bytes 200000 | tf_op jit(solution)/shard_map/pallas_call | solution.py:217
  26.1 9.7 %all-to-all-done.spec_ref = bf16[128,8,512]{2,1,0:T(8,128)(2,1)S(1)} async-done(((bf16[128,8,512]{2,1,0:T(8,128)(2,1)}), bf16[128,8,512]{2,1,0:T(8,128)(2,1)S(1)}, u32[]{:S(2)}, u32[]{:S(2)}) %all-to-all-start) | async-done | bytes 1048608 | tf_op jit(solution)/shard_map/all_to_all | solution.py:456
  35.7 6.6 %shard_map.66 = bf16[128,72,128]{2,1,0:T(8,128)(2,1)} custom-call(bf16[128,128,128]{2,1,0:T(8,128)(2,1)} %get-tuple-element.8.chosen_hbm, s32[8,128]{1,0:T(8,128)S(1)} %get-tuple-element.9.shift_ref, bf16[128,8,512]{2,1,0:T(8,128)(2,1)S(1)} %all-to-all-done.spec_ref), custom_call_target="tpu_custom_call" | custom-call | tf_op jit(solution)/shard_map/pallas_call | solution.py:387
  42.3 0.0 copy-start
  42.3 4.4 %all-to-all-start.1 = ((bf16[128,72,128]{2,1,0:T(8,128)(2,1)}), bf16[128,72,128]{2,1,0:T(8,128)(2,1)S(1)}, u32[]{:S(2)}, u32[]{:S(2)}) async-start(bf16[128,72,128]{2,1,0:T(8,128)(2,1)} %shard_map.66), calls=%async_computation.1 | async-start | bytes 4718592 | tf_op jit(solution)/shard_map/all_to_all | solution.py:459
  46.7 32.4 %all-to-all-done.1.cross_ref = bf16[128,72,128]{2,1,0:T(8,128)(2,1)S(1)} async-done(((bf16[128,72,128]{2,1,0:T(8,128)(2,1)}), bf16[128,72,128]{2,1,0:T(8,128)(2,1)S(1)}, u32[]{:S(2)}, u32[]{:S(2)}) %all-to-all-start.1) | async-done | bytes 2359328 | tf_op jit(solution)/shard_map/all_to_all | solution.py:459
  79.1 0.0 copy-done
  79.1 3.4 %shard_map.67 = f32[3,3,128,512]{3,2,1,0:T(8,128)} custom-call(s32[1]{0:T(128)} %bitcast.owner_ref, bf16[128,72,128]{2,1,0:T(8,128)(2,1)S(1)} %all-to-all-done.1.cross_ref, bf16[1024,512]{1,0:T(8,128)(2,1)S(1)} %copy-done, s32[128,128]{1,0:T(8,128)S(1)} %get-tuple-element.10.place_ref, f32[3,3,128,512]{3,2,1,0:T(8,128)} %bitcast.11), custom_call_target="tpu_custom_call" | custom-call | tf_op jit(solution)/shard_map/pallas_call | solution.py:436
Async XLA Ops:
  0.0 16.4 %copy-start.1 = (s32[128,128]{1,0:T(8,128)S(1)}, s32[128,128]{1,0:T(8,128)}, u32[]{:S(2)}) copy-start(s32[128,128]{1,0:T(8,128)} %param.8) | copy-start | bytes 196612
  4.9 30.8 %all-to-all-start = ((bf16[128,8,512]{2,1,0:T(8,128)(2,1)}), bf16[128,8,512]{2,1,0:T(8,128)(2,1)S(1)}, u32[]{:S(2)}, u32[]{:S(2)}) async-start(bf16[128,8,512]{2,1,0:T(8,128)(2,1)} %shard_map.65), calls=%async_computation | async-start | bytes 2097152 | tf_op jit(solution)/shard_map/all_to_all | solution.py:456
  42.3 36.8 %copy-start = (bf16[1024,512]{1,0:T(8,128)(2,1)S(1)}, bf16[1024,512]{1,0:T(8,128)(2,1)}, u32[]{:S(2)}) copy-start(bf16[1024,512]{1,0:T(8,128)(2,1)} %constant.16.clone.table_ref) | copy-start | bytes 3145732
  42.3 36.8 %all-to-all-start.1 = ((bf16[128,72,128]{2,1,0:T(8,128)(2,1)}), bf16[128,72,128]{2,1,0:T(8,128)(2,1)S(1)}, u32[]{:S(2)}, u32[]{:S(2)}) async-start(bf16[128,72,128]{2,1,0:T(8,128)(2,1)} %shard_map.66), calls=%async_computation.1 | async-start | bytes 4718592 | tf_op jit(solution)/shard_map/all_to_all | solution.py:459

commit v7 on v6

--- a/solution.py
+++ b/solution.py
@@ -111,8 +111,10 @@
     power = real * real + imag * imag
     high = power.astype(jnp.bfloat16)
     low = (power - high.astype(jnp.float32)).astype(jnp.bfloat16)
-    smooth = jnp.dot(near, high, preferred_element_type=jnp.float32) + jnp.dot(
-        near, low, preferred_element_type=jnp.float32
+    smooth = jnp.dot(
+        jnp.concatenate([near, near], axis=1),
+        jnp.concatenate([high, low], axis=0),
+        preferred_element_type=jnp.float32,
     )
     bin_id = bin_of(lax.broadcasted_iota(jnp.int32, (FREQ_BINS, 1), 0))
     width = jnp.minimum(bin_id, BAND_HALF) + jnp.minimum(FREQ_BINS - 1 - bin_id, BAND_HALF) + 1
@@ -412,14 +414,21 @@
     row = lax.broadcasted_iota(jnp.int32, (PER_OWNER, PER_OWNER), 0)
     chosen = jnp.where(row == place_ref[pl.ds(owner_ref[0], 1), :], 1.0, 0.0).astype(jnp.bfloat16)
     new_copies = []
-    for c in range(COMPONENTS):
+    def turn(c):
         rows = []
         for d in range(COMPONENTS):
             begin = (c * COMPONENTS + d) * PARTS
             spectra = cross_ref[:, begin : begin + PARTS, :].reshape(2 * FREQ_BINS, PER_OWNER)
             turned = lax.dot_general(chosen, spectra, NT, preferred_element_type=jnp.float32)
             rows.append(turned.astype(jnp.bfloat16))
-        lagged = jnp.dot(jnp.concatenate(rows, axis=0), table_ref[...], preferred_element_type=jnp.float32)
+        return jnp.concatenate(rows, axis=0)
+
+    ahead = turn(0)
+    for c in range(COMPONENTS):
+        rows = ahead
+        if c + 1 < COMPONENTS:
+            ahead = turn(c + 1)
+        lagged = jnp.dot(rows, table_ref[...], preferred_element_type=jnp.float32)
         new[c] = lagged.reshape(COMPONENTS, PER_OWNER, LAG_BINS)
         for e in ((), (0, 1), (2,))[c]:
             for d in range(COMPONENTS):

time: 82.7 us -> 82.7 us (level)
  no operation moved by 1% of the time
where the time goes in v7:
time: 82.7 us; the launch traced here: 82.5 us
  waiting for transfers between devices  42 us (51%)
  Pallas kernels  23.7 us (29%)
  starting transfers between devices  15.9 us (19%)
    all_to_all x1, waiting for transfers between devices, local(): lax.all_to_all(crossed, axes, split_axis=0, concat_axis=0, tiled=True)  32.4 us
    all_to_all x1, starting transfers between devices, local(): lax.all_to_all(spectra, axes, split_axis=0, concat_axis=0, tiled=True)  11.5 us
    all_to_all x1, waiting for transfers between devices, local(): lax.all_to_all(spectra, axes, split_axis=0, concat_axis=0, tiled=True)  9.65 us
    pallas_call x1, Pallas kernels, route(): pl.pallas_call(route_kernel, out_shape=(pltpu.HBM((DEVICES, PER_OWNER, PE...  8.83 us
    pallas_call x1, Pallas kernels, cross(): pl.pallas_call(cross_kernel, out_shape=pltpu.HBM((DEVICES, VALUES, PER_OW...  6.59 us
    pallas_call x1, Pallas kernels, whiten(): pl.pallas_call(whiten_kernel, out_shape=pltpu.HBM((DEVICES, PARTS, LANES_...  4.87 us
    all_to_all x1, starting transfers between devices, local(): lax.all_to_all(crossed, axes, split_axis=0, concat_axis=0, tiled=True)  4.42 us
    pallas_call x1, Pallas kernels, lag(): pl.pallas_call(lag_kernel, out_shape=pltpu.HBM(old_rows.shape, jnp.float3...  3.38 us
  transfers between devices with their start and end apart: 2, of which 2 were waited for; matrix products, arithmetic and copies ran while one was open for 1% of the time, Pallas kernels for 11%

profile of v7, /device:TPU:1, one launch (start us, length us, event | category | flops | bytes accessed | tf_op | source)
XLA Modules:
  0.0 82.5 jit_solution(2004158064627618254)
XLA Ops:
  0.0 0.0 copy-start.1
  0.0 4.9 %shard_map.65 = bf16[128,8,512]{2,1,0:T(8,128)(2,1)} custom-call(s32[1,2]{1,0:T(1,128)} %avail_hbm.1, bf16[480,1024]{1,0:T(8,128)(2,1)} %bitcast.13, bf16[528,1024]{1,0:T(8,128)(2,1)} %constant.15.clone.dft_hbm), custom_call_target="tpu_custom_call" | custom-call | tf_op jit(solution)/shard_map/pallas_call | solution.py:146
  4.9 11.5 %all-to-all-start = ((bf16[128,8,512]{2,1,0:T(8,128)(2,1)}), bf16[128,8,512]{2,1,0:T(8,128)(2,1)S(1)}, u32[]{:S(2)}, u32[]{:S(2)}) async-start(bf16[128,8,512]{2,1,0:T(8,128)(2,1)} %shard_map.65), calls=%async_computation | async-start | bytes 2097152 | tf_op jit(solution)/shard_map/all_to_all | solution.py:465
  16.4 0.0 copy-done.1
  16.4 0.2 reshape.13
  16.6 0.3 copy.11
  16.9 0.2 reshape.14
  17.1 0.1 copy.9.slot_ref
  17.2 8.8 %shard_map.64 = (bf16[128,128,128]{2,1,0:T(8,128)(2,1)}, s32[128,128]{1,0:T(8,128)S(1)}, s32[8,128]{1,0:T(8,128)S(1)}) custom-call(s32[128,128]{1,0:T(8,128)S(1)} %copy.9.slot_ref), custom_call_target="tpu_custom_call" | custom-call | flops 40000000 | bytes 200000 | tf_op jit(solution)/shard_map/pallas_call | solution.py:219
  26.0 9.7 %all-to-all-done.spec_ref = bf16[128,8,512]{2,1,0:T(8,128)(2,1)S(1)} async-done(((bf16[128,8,512]{2,1,0:T(8,128)(2,1)}), bf16[128,8,512]{2,1,0:T(8,128)(2,1)S(1)}, u32[]{:S(2)}, u32[]{:S(2)}) %all-to-all-start) | async-done | bytes 1048608 | tf_op jit(solution)/shard_map/all_to_all | solution.py:465
  35.7 6.6 %shard_map.66 = bf16[128,72,128]{2,1,0:T(8,128)(2,1)} custom-call(bf16[128,128,128]{2,1,0:T(8,128)(2,1)} %get-tuple-element.8.chosen_hbm, s32[8,128]{1,0:T(8,128)S(1)} %get-tuple-element.9.shift_ref, bf16[128,8,512]{2,1,0:T(8,128)(2,1)S(1)} %all-to-all-done.spec_ref), custom_call_target="tpu_custom_call" | custom-call | tf_op jit(solution)/shard_map/pallas_call | solution.py:389
  42.3 0.0 copy-start
  42.3 4.4 %all-to-all-start.1 = ((bf16[128,72,128]{2,1,0:T(8,128)(2,1)}), bf16[128,72,128]{2,1,0:T(8,128)(2,1)S(1)}, u32[]{:S(2)}, u32[]{:S(2)}) async-start(bf16[128,72,128]{2,1,0:T(8,128)(2,1)} %shard_map.66), calls=%async_computation.1 | async-start | bytes 4718592 | tf_op jit(solution)/shard_map/all_to_all | solution.py:468
  46.7 32.4 %all-to-all-done.1.cross_ref = bf16[128,72,128]{2,1,0:T(8,128)(2,1)S(1)} async-done(((bf16[128,72,128]{2,1,0:T(8,128)(2,1)}), bf16[128,72,128]{2,1,0:T(8,128)(2,1)S(1)}, u32[]{:S(2)}, u32[]{:S(2)}) %all-to-all-start.1) | async-done | bytes 2359328 | tf_op jit(solution)/shard_map/all_to_all | solution.py:468
  79.1 0.0 copy-done
  79.1 3.4 %shard_map.67 = f32[3,3,128,512]{3,2,1,0:T(8,128)} custom-call(s32[1]{0:T(128)} %bitcast.owner_ref, bf16[128,72,128]{2,1,0:T(8,128)(2,1)S(1)} %all-to-all-done.1.cross_ref, bf16[1024,512]{1,0:T(8,128)(2,1)S(1)} %copy-done, s32[128,128]{1,0:T(8,128)S(1)} %get-tuple-element.10.place_ref, f32[3,3,128,512]{3,2,1,0:T(8,128)} %bitcast.11), custom_call_target="tpu_custom_call" | custom-call | tf_op jit(solution)/shard_map/pallas_call | solution.py:445
Async XLA Ops:
  0.0 16.4 %copy-start.1 = (s32[128,128]{1,0:T(8,128)S(1)}, s32[128,128]{1,0:T(8,128)}, u32[]{:S(2)}) copy-start(s32[128,128]{1,0:T(8,128)} %param.8) | copy-start | bytes 196612
  4.9 30.8 %all-to-all-start = ((bf16[128,8,512]{2,1,0:T(8,128)(2,1)}), bf16[128,8,512]{2,1,0:T(8,128)(2,1)S(1)}, u32[]{:S(2)}, u32[]{:S(2)}) async-start(bf16[128,8,512]{2,1,0:T(8,128)(2,1)} %shard_map.65), calls=%async_computation | async-start | bytes 2097152 | tf_op jit(solution)/shard_map/all_to_all | solution.py:465
  42.3 36.8 %copy-start = (bf16[1024,512]{1,0:T(8,128)(2,1)S(1)}, bf16[1024,512]{1,0:T(8,128)(2,1)}, u32[]{:S(2)}) copy-start(bf16[1024,512]{1,0:T(8,128)(2,1)} %constant.16.clone.table_ref) | copy-start | bytes 3145732
  42.3 36.8 %all-to-all-start.1 = ((bf16[128,72,128]{2,1,0:T(8,128)(2,1)}), bf16[128,72,128]{2,1,0:T(8,128)(2,1)S(1)}, u32[]{:S(2)}, u32[]{:S(2)}) async-start(bf16[128,72,128]{2,1,0:T(8,128)(2,1)} %shard_map.66), calls=%async_computation.1 | async-start | bytes 4718592 | tf_op jit(solution)/shard_map/all_to_all | solution.py:468
